TPU v7x, 512 devices: a whole 4x4x16 slice. The times are simulated.
512 devices in a mesh: head: 4 (over y_lo, core), qctx: 16 (over z), kctx: 8 (over x, y_hi).
Axes of the slice: x: 4, y: 4 (y_hi: 2, y_lo: 2; y = y_hi * 2 + y_lo), z: 16, core: 2. Of those that a mesh axis runs over, the one named last changes fastest.
Arguments:
- queries: bfloat16 [24576, 8192], P(('qctx', 'kctx'), 'head'), may hold values from -40 to 40
- keys: bfloat16 [24576, 512], P(('qctx', 'kctx'), 'head'), may hold values from -40 to 40
- values: bfloat16 [24576, 512], P(('qctx', 'kctx'), 'head'), may hold values from -6 to 6
- doc_lengths: int32 [16], replicated, may hold values from 1 to 3072, 24576 in all
Outputs:
- attended: bfloat16 [24576, 8192], P(('qctx', 'kctx'), 'head')
Inputs may be any that keep to these rules, and one draw needn't show every extreme that they name: `doc_lengths`: every document holds at most 3072 tokens and one holds exactly 3072; the lengths sum to 24576.
All inputs are finite; a program needn't handle non-finite values.
Results may differ from a plain program's by a relative error of at most 0.0049.
Values may be sent and summed in bfloat16 or wider, within the bound.
No kernel may reach another device: no remote copies, remote signals or barrier semaphores. Data moves between devices by JAX's collectives and lax.ppermute only.
A program may use at most 64 MiB of HBM per device.

v0:
```python
from functools import partial

import jax
import jax.numpy as jnp
from jax import lax
from jax.sharding import PartitionSpec as P

HD = 128
REACH = 2


def passed_along(x, axis, by):
    count = lax.axis_size(axis)
    pairs = [(i, i + by) for i in range(count) if 0 <= i + by < count]
    return lax.ppermute(x, axis, pairs)


def earlier(current):
    pieces = [current]
    moving = current
    for offset in range(REACH):
        moving = passed_along(moving, "qctx", 1)
        pieces.append(moving)
    return pieces


def attend(state, kv_rows, key_start, queries_split, query_pos, doc_first, kv_heads):
    top_score, totals, accum = state
    block_rows = kv_rows.shape[0]
    key_rows = kv_rows[:, : kv_heads * HD].reshape(block_rows, kv_heads, HD)
    value_rows = kv_rows[:, kv_heads * HD :].reshape(block_rows, kv_heads, HD)
    scores = jnp.einsum(
        "qcgd,kcd->cgqk", queries_split, key_rows, preferred_element_type=jnp.float32
    ) * HD ** (-0.5)
    key_pos = key_start + jnp.arange(block_rows, dtype=jnp.int32)
    allowed = (key_pos[None, :] >= doc_first[:, None]) & (key_pos[None, :] <= query_pos[:, None])
    masked = jnp.where(allowed, scores, jnp.float32(-1e30))
    new_top = jnp.maximum(top_score, jnp.max(masked, axis=-1))
    correction = jnp.exp(top_score - new_top)
    weights = jnp.where(allowed, jnp.exp(scores - new_top[..., None]), jnp.float32(0.0))
    totals = totals * correction + jnp.sum(weights, axis=-1)
    update = jnp.einsum(
        "cgqk,kcd->cgqd",
        weights.astype(jnp.bfloat16),
        value_rows,
        preferred_element_type=jnp.float32,
    )
    accum = accum * correction[..., None] + update
    return (new_top, totals, accum)


def keep_state(state):
    return state


def shards(queries, keys, values, doc_lengths):
    fine_rows = queries.shape[0]
    kv_heads = keys.shape[1] // HD
    group_count = queries.shape[1] // (kv_heads * HD)
    block_rows = fine_rows * lax.axis_size("kctx")
    block_index = lax.axis_index("qctx")
    row_index = block_index * lax.axis_size("kctx") + lax.axis_index("kctx")
    query_pos = row_index * fine_rows + jnp.arange(fine_rows, dtype=jnp.int32)
    starts = jnp.cumsum(doc_lengths) - doc_lengths
    doc_first = jnp.max(
        jnp.where(starts[None, :] <= query_pos[:, None], starts[None, :], 0), axis=1
    )
    fine_kv = jnp.concatenate([keys, values], axis=1)
    middle = lax.all_gather(fine_kv, "kctx", axis=0, tiled=True)
    pieces = earlier(middle)
    queries_split = queries.reshape(fine_rows, kv_heads, group_count, HD)
    state = (
        jnp.full((kv_heads, group_count, fine_rows), -1e30, jnp.float32),
        jnp.zeros((kv_heads, group_count, fine_rows), jnp.float32),
        jnp.zeros((kv_heads, group_count, fine_rows, HD), jnp.float32),
    )
    for offset in range(REACH + 1):
        key_start = (block_index - offset) * block_rows
        live_block = (key_start + block_rows > doc_first[0]) & (key_start <= query_pos[-1])
        step_fn = partial(
            attend,
            kv_rows=pieces[offset],
            key_start=key_start,
            queries_split=queries_split,
            query_pos=query_pos,
            doc_first=doc_first,
            kv_heads=kv_heads,
        )
        state = lax.cond(live_block, step_fn, keep_state, state)
    result = state[2] / state[1][..., None]
    result = jnp.transpose(result, (2, 0, 1, 3)).reshape(fine_rows, kv_heads * group_count * HD)
    return result.astype(jnp.bfloat16)


def solution(mesh):
    placed = (
        P(("qctx", "kctx"), "head"),
        P(("qctx", "kctx"), "head"),
        P(("qctx", "kctx"), "head"),
        P(),
    )
    return jax.shard_map(
        shards, mesh=mesh, in_specs=placed, out_specs=P(("qctx", "kctx"), "head"), check_vma=False
    )
```

profile of v0, /device:TPU:248, one launch (start us, length us, event | category | flops | bytes accessed | tf_op | source)
XLA Modules:
  0.0 155.9 jit_solution(9447826338323691620)
XLA Ops:
  0.0 0.8 pad_maximum_fusion
  0.8 36.1 %all_gather.3 = bf16[1536,256]{1,0:T(8,128)(2,1)S(1)} all-gather(bf16[192,256]{1,0:T(8,128)(2,1)S(1)} %pad_maximum_fusion), channel_id=1, replica_groups=mesh['head'=4,'qctx'=16,'kctx'=8] {'kctx'}, dimensions={0}, use_global_device_ids=true | all-gather | bytes 884736 | tf_op jit(solution)/shard_map/all_gather | solution.py:69
  36.9 5.0 %collective-permute-start = (bf16[1536,256]{1,0:T(8,128)(2,1)S(1)}, bf16[1536,256]{1,0:T(8,128)(2,1)}, u32[]{:S(2)}, u32[]{:S(2)}) collective-permute-start(bf16[1536,256]{1,0:T(8,128)(2,1)S(1)} %all_gather.3), channel_id=1, source_target_pairs={{0,8},{8,16},{16,24},{24,32},{32,40},{40,48},{48,56},{56,64},{64,7... | collective-permute-start | bytes 2359304 | tf_op jit(solution)/shard_map/ppermute | solution.py:15
  42.0 11.9 %collective-permute-done = bf16[1536,256]{1,0:T(8,128)(2,1)} collective-permute-done((bf16[1536,256]{1,0:T(8,128)(2,1)S(1)}, bf16[1536,256]{1,0:T(8,128)(2,1)}, u32[]{:S(2)}, u32[]{:S(2)}) %collective-permute-start) | collective-permute-done | bytes 786464 | tf_op jit(solution)/shard_map/ppermute | solution.py:15
  53.9 5.6 %collective-permute-start.1 = (bf16[1536,256]{1,0:T(8,128)(2,1)}, bf16[1536,256]{1,0:T(8,128)(2,1)}, u32[]{:S(2)}, u32[]{:S(2)}) collective-permute-start(bf16[1536,256]{1,0:T(8,128)(2,1)} %collective-permute-done), channel_id=1, source_target_pairs={{0,8},{8,16},{16,24},{24,32},{32,40},{40,48},{48,56},{56,64},{64,7... | collective-permute-start | bytes 2359304 | tf_op jit(solution)/shard_map/ppermute | solution.py:15
  59.5 0.7 slice.29
  62.2 0.7 copy.12
  63.0 0.1 reduce.6
  63.1 0.7 sub.62
  63.8 0.1 select_reduce_fusion
  63.9 0.6 slice.28
  66.6 1.3 copy.17
  67.9 27.9 %conditional.3 = (f32[1,16,192]{2,1,0:T(8,128)S(1)}, f32[1,16,192]{2,1,0:T(8,128)S(1)}, f32[1,16,192,128]{3,2,1,0:T(8,128)S(1)}) conditional(s32[]{:T(128)} %convert_element_type.29, () %tuple.26, (s32[]{:T(128)}, s32[192]{0:T(256)S(1)}, s32[192]{0:T(256)S(1)}, bf16[1536,256]{1,0:T(8,128)(2,1)S(1)}, bf16[192,1,16,128]{3,2,0,1:T(8,128)(2,1)S(1)}) %tuple.54), branch_computations={%region_2.3_spmd, %region_3.6_spmd} | conditional | flops 2469118464 | bytes 61117980 | solution.py:89
  67.9 0.3 compare_and_fusion
  68.2 8.5 %fusion = (f32[16,192]{1,0:T(8,128)S(1)}, f32[1536,192,16]{0,1,2:T(8,128)}) fusion(pred[192,1536]{1,0:T(8,128)(4,1)S(1)} %compare_and_fusion, bf16[192,1,16,128]{3,2,0,1:T(8,128)(2,1)S(1)} %get-tuple-element.119, bf16[1536,256]{1,0:T(8,128)(2,1)S(1)} %get-tuple-element.60), kind=kOutput, calls=%fused_computation.2 | convolution fusion | flops 1222112256 | bytes 20361216 | tf_op jit(solution)/shard_map/cond/branch_1_fun/qcgd,kcd->cgqk/dot_general | solution.py:32
  76.8 10.7 %fusion.4 = f32[16,192]{1,0:T(8,128)S(1)} fusion(f32[1536,192,16]{0,1,2:T(8,128)} %get-tuple-element.147, f32[16,192]{1,0:T(8,128)S(1)} %get-tuple-element.145, pred[192,1536]{1,0:T(8,128)(4,1)S(1)} %compare_and_fusion), kind=kLoop, calls=%fused_computation.6 | loop fusion | flops 18871296 | bytes 19193856 | tf_op jit(solution)/shard_map/cond/branch_1_fun/reduce_sum | solution.py:41
  87.5 8.3 %add_bitcast_fusion = f32[1,16,192,128]{3,2,1,0:T(8,128)S(1)} fusion(f32[1536,192,16]{0,1,2:T(8,128)} %get-tuple-element.147, f32[16,192]{1,0:T(8,128)S(1)} %get-tuple-element.145, pred[192,1536]{1,0:T(8,128)(4,1)S(1)} %compare_and_fusion, f32[16,192]{1,0:T(8,128)S(1)} %get-tuple-element.144, bf16[1536,256]{1,0:T(8,128)(2,1)S(1)} %get-tuple-element.60), kind=kOutput, calls=%fused_computation.10 | convolution fusion | flops 1227227136 | bytes 21168128 | tf_op jit(solution)/shard_map/cond/branch_1_fun/cgqk,kcd->cgqd/dot_general | solution.py:42
  95.8 29.0 %conditional.4 = ((f32[1,16,192]{2,1,0:T(8,128)S(1)}, f32[1,16,192]{2,1,0:T(8,128)S(1)}, f32[1,16,192,128]{3,2,1,0:T(8,128)S(1)})) conditional(s32[]{:T(128)} %convert_element_type.28, (f32[1,16,192]{2,1,0:T(8,128)S(1)}, f32[1,16,192]{2,1,0:T(8,128)S(1)}, f32[1,16,192,128]{3,2,1,0:T(8,128)S(1)}) %conditional.3, (s32[]{:T(128)}, s32[192]{0:T(256)S(1)}, ...), branch_computations={%region_6.7_spmd, %region_7.10_spmd} | conditional | flops 2469505536 | bytes 62731812 | solution.py:89
  96.0 0.3 compare_and_fusion.1
  96.3 9.3 %fusion.21 = (f32[16,192]{1,0:T(8,128)S(1)}, f32[1536,192,16]{0,1,2:T(8,128)}) fusion(pred[192,1536]{1,0:T(8,128)(4,1)S(1)} %compare_and_fusion.1, bf16[192,1,16,128]{3,2,0,1:T(8,128)(2,1)S(1)} %get-tuple-element.124, bf16[1536,256]{1,0:T(8,128)(2,1)} %get-tuple-element.66), kind=kOutput, calls=%fused_computation.28 | convolution fusion | flops 1222112256 | bytes 20361216 | tf_op jit(solution)/shard_map/cond/branch_1_fun/qcgd,kcd->cgqk/dot_general | solution.py:32
  105.6 10.7 %fusion.25 = f32[16,192]{1,0:T(8,128)S(1)} fusion(f32[1536,192,16]{0,1,2:T(8,128)} %get-tuple-element.149, f32[16,192]{1,0:T(8,128)S(1)} %bitcast.171, pred[192,1536]{1,0:T(8,128)(4,1)S(1)} %compare_and_fusion.1), kind=kLoop, calls=%fused_computation.32 | loop fusion | flops 18871296 | bytes 19193856 | tf_op jit(solution)/shard_map/cond/branch_1_fun/reduce_sum | solution.py:41
  116.3 8.4 %bitcast_add_fusion.1 = f32[1,16,192,128]{3,2,1,0:T(8,128)S(1)} fusion(f32[1,16,192,128]{3,2,1,0:T(8,128)S(1)} %get-tuple-element.69, f32[1536,192,16]{0,1,2:T(8,128)} %get-tuple-element.149, f32[16,192]{1,0:T(8,128)S(1)} %bitcast.172, pred[192,1536]{1,0:T(8,128)(4,1)S(1)} %compare_and_fusion.1, f32[16,192]{1,0:T(8,128)S(1)} %get-tuple-element.138, ...), kind=kOutput, calls=%fused_computation.36 | convolution fusion | flops 1227620352 | bytes 22732800 | tf_op jit(solution)/shard_map/cond/branch_1_fun/cgqk,kcd->cgqd/dot_general | solution.py:42
  124.7 0.0 collective-permute-done.1
  124.8 29.0 %conditional.5 = ((f32[1,16,192]{2,1,0:T(8,128)S(1)}, f32[1,16,192,128]{3,2,1,0:T(8,128)S(1)})) conditional(s32[]{:T(128)} %convert_element_type.27, (f32[1,16,192]{2,1,0:T(8,128)S(1)}, f32[1,16,192,128]{3,2,1,0:T(8,128)S(1)}) %tuple.29, (s32[]{:T(128)}, s32[192]{0:T(256)S(1)}, s32[192]{0:T(256)S(1)}, bf16[1536,256]{1,0:T(8,128)(2,1)}, ...), branch_computations={%region_10.11_spmd, %region_11.14_spmd} | conditional | flops 2469508608 | bytes 62707228 | solution.py:89
  125.0 0.3 compare_and_fusion.2
  125.3 9.3 %fusion.42 = (f32[16,192]{1,0:T(8,128)S(1)}, f32[1536,192,16]{0,1,2:T(8,128)}) fusion(pred[192,1536]{1,0:T(8,128)(4,1)S(1)} %compare_and_fusion.2, bf16[192,1,16,128]{3,2,0,1:T(8,128)(2,1)S(1)} %get-tuple-element.132, bf16[1536,256]{1,0:T(8,128)(2,1)} %get-tuple-element.75), kind=kOutput, calls=%fused_computation.54 | convolution fusion | flops 1222112256 | bytes 20361216 | tf_op jit(solution)/shard_map/cond/branch_1_fun/qcgd,kcd->cgqk/dot_general | solution.py:32
  134.7 10.7 %fusion.46 = f32[16,192]{1,0:T(8,128)S(1)} fusion(f32[1536,192,16]{0,1,2:T(8,128)} %get-tuple-element.143, f32[16,192]{1,0:T(8,128)S(1)} %get-tuple-element.141, pred[192,1536]{1,0:T(8,128)(4,1)S(1)} %compare_and_fusion.2), kind=kLoop, calls=%fused_computation.58 | loop fusion | flops 18871296 | bytes 19193856 | tf_op jit(solution)/shard_map/cond/branch_1_fun/reduce_sum | solution.py:41
  145.4 8.4 %bitcast_add_fusion.3 = f32[1,16,192,128]{3,2,1,0:T(8,128)S(1)} fusion(f32[1,16,192,128]{3,2,1,0:T(8,128)S(1)} %get-tuple-element.77, f32[1536,192,16]{0,1,2:T(8,128)} %get-tuple-element.143, f32[16,192]{1,0:T(8,128)S(1)} %get-tuple-element.141, pred[192,1536]{1,0:T(8,128)(4,1)S(1)} %compare_and_fusion.2, f32[16,192]{1,0:T(8,128)S(1)} %get-tuple-element.140, ...), kind=kOutput, calls=%fused_computation.62 | convolution fusion | flops 1227620352 | bytes 22732800 | tf_op jit(solution)/shard_map/cond/branch_1_fun/cgqk,kcd->cgqd/dot_general | solution.py:42
  153.8 0.5 fusion.64
  154.2 0.5 copy.16
  154.8 1.1 copy.38
  (12 shorter events, 0.1 us)
Async XLA Ops:
  36.9 17.0 %collective-permute-start = (bf16[1536,256]{1,0:T(8,128)(2,1)S(1)}, bf16[1536,256]{1,0:T(8,128)(2,1)}, u32[]{:S(2)}, u32[]{:S(2)}) collective-permute-start(bf16[1536,256]{1,0:T(8,128)(2,1)S(1)} %all_gather.3), channel_id=1, source_target_pairs={{0,8},{8,16},{16,24},{24,32},{32,40},{40,48},{48,56},{56,64},{64,7... | collective-permute-start | bytes 2359304 | tf_op jit(solution)/shard_map/ppermute | solution.py:15
  53.9 70.8 %collective-permute-start.1 = (bf16[1536,256]{1,0:T(8,128)(2,1)}, bf16[1536,256]{1,0:T(8,128)(2,1)}, u32[]{:S(2)}, u32[]{:S(2)}) collective-permute-start(bf16[1536,256]{1,0:T(8,128)(2,1)} %collective-permute-done), channel_id=1, source_target_pairs={{0,8},{8,16},{16,24},{24,32},{32,40},{40,48},{48,56},{56,64},{64,7... | collective-permute-start | bytes 2359304 | tf_op jit(solution)/shard_map/ppermute | solution.py:15
where the time goes:
time: 156 us
  matrix products  52.3 us (34%)
  blocking collectives  36.1 us (23%)
  other arithmetic  35.3 us (23%)
  waiting for transfers between devices  11.9 us (8%)
  starting transfers between devices  10.6 us (7%)
  local copies, waits for them, and re-layouts  4.88 us (3%)
  between operations  4.27 us (3%)
    all_gather x1, blocking collectives, shards(): middle = lax.all_gather(fine_kv, 'kctx', axis=0, tiled=True)  36.1 us
    reduce_sum x3, other arithmetic, attend(): totals = totals * correction + jnp.sum(weights, axis=-1)  32 us
    dot_general x3, matrix products, attend(): jnp.einsum('qcgd,kcd->cgqk', queries_split, key_rows, preferred_element_t...  27.2 us
    dot_general x3, matrix products, attend(): jnp.einsum('cgqk,kcd->cgqd', weights.astype(jnp.bfloat16), value_rows, pr...  25.1 us
    ppermute x2, waiting for transfers between devices, passed_along(): return lax.ppermute(x, axis, pairs)  11.9 us
    ppermute x2, starting transfers between devices, passed_along(): return lax.ppermute(x, axis, pairs)  10.6 us
  transfers between devices with their start and end apart: 2, of which 1 were waited for; matrix products, arithmetic and copies ran while one was open for 39% of the time, Pallas kernels for 0%

commit v1 on v0

v1 whole, which is shorter than its diff:
```python
from functools import partial

import jax
import jax.numpy as jnp
from jax import lax
from jax.experimental import pallas as pl
from jax.experimental.pallas import tpu as pltpu
from jax.sharding import PartitionSpec as P

HD = 128
STEP = 4
SUB = 2
TILE = 512
SCALE = HD**-0.5 * 1.4426950408889634
SAFE = 100.0
FAR = -(2.0**100)

bf16 = jnp.bfloat16
f32 = jnp.float32


def product(a, b, dims):
    return lax.dot_general(a, b, (dims, ((), ())), preferred_element_type=f32)


def largest_norm(x):
    squares = (x.astype(f32) * x.astype(f32)).astype(bf16)
    sums = product(squares, jnp.ones((HD, HD), bf16), ((1,), (0,)))
    return jnp.max(sums) * 1.02


def kernel(first, last, *refs):
    if first:
        place, docs, q_ref, kv_ref, out_ref, plain_out, norm_out, kx, vx, qx, knorm = refs
    elif last:
        place, plain_in, norm_in, docs, q_ref, kv_ref, state_ref, out_ref, kx, vx, qx, knorm = refs
    else:
        place, plain_in, norm_in, docs, q_ref, kv_ref, state_ref, out_ref, plain_out, kx, vx, qx, knorm = refs
    step = pl.program_id(0)
    keys = kv_ref.shape[0]
    rows = q_ref.shape[0]
    tile = min(TILE, keys)
    starts, ends = docs[0:1, :], docs[1:2, :]

    @pl.when(step == 0)
    def _():
        kx[:, 0:HD] = kv_ref[:, 0:HD]
        vx[:, 0:HD] = kv_ref[:, HD:]
        at = lax.broadcasted_iota(jnp.int32, (keys, HD), 0)
        pos = place[1] + at - jnp.where(at >= place[2], place[3], 0)
        kx[:, HD:] = jnp.where((pos >= starts) & (pos < ends), 0.0, FAR).astype(bf16)
        vx[:, HD:] = jnp.ones((keys, HD), bf16)
        at = lax.broadcasted_iota(jnp.int32, (rows, HD), 0) + place[0]
        own = jnp.where((at >= starts) & (at < ends), 1.0, 0.0).astype(bf16)
        for h in range(STEP):
            qx[h * rows : (h + 1) * rows, HD:] = own
        knorm[0] = largest_norm(kv_ref[:, 0:HD])

    for h in range(STEP):
        qx[h * rows : (h + 1) * rows, 0:HD] = q_ref[:, h * HD : (h + 1) * HD]
    if first:
        qnorm = largest_norm(qx[:, 0:HD])
        norm_out[step] = qnorm
    else:
        qnorm = norm_in[step]
    plain = qnorm * knorm[0] <= (SAFE / SCALE) ** 2
    if not first:
        plain = plain & (plain_in[step] == 1)
    if not last:
        plain_out[step] = plain.astype(jnp.int32)

    def scores(q, k):
        s = product(q, k, ((1,), (1,))) * SCALE
        if first:
            heads = q.shape[0] // rows
            r = lax.broadcasted_iota(jnp.int32, (rows, keys), 0)
            c = lax.broadcasted_iota(jnp.int32, (rows, keys), 1)
            early = jnp.concatenate([c <= r] * heads, axis=0)
            s = jnp.where(early, s, FAR)
        return s

    def put(row, state):
        if last:
            for h in range(state.shape[0] // rows):
                part = state[h * rows : (h + 1) * rows]
                out = part[:, 0:HD] / jnp.broadcast_to(part[:, HD : HD + 1], (rows, HD))
                head = row // rows + h
                if isinstance(row, int):
                    out_ref[:, head * HD : (head + 1) * HD] = out.astype(bf16)
                else:
                    out_ref[:, pl.ds(pl.multiple_of(head * HD, HD), HD)] = out.astype(bf16)
        else:
            out_ref[pl.ds(row, state.shape[0]), :] = state

    @pl.when(plain)
    def _():
        size = SUB * rows
        for row in range(0, STEP * rows, size):
            state = None if first else state_ref[row : row + size, :]
            for key in range(0, keys, tile):
                s = scores(qx[row : row + size, :], kx[key : key + tile, :])
                update = product(jnp.exp2(s).astype(bf16), vx[key : key + tile, :], ((1,), (0,)))
                state = update if state is None else state + update
            if first:
                lane = lax.broadcasted_iota(jnp.int32, state.shape, 1)
                state = jnp.where(lane == 2 * HD - 1, 0.0, state)
            put(row, state)

    @pl.when(jnp.logical_not(plain))
    def _():
        def head(h, carry):
            row = pl.multiple_of(h * rows, rows)
            lane = lax.broadcasted_iota(jnp.int32, (rows, 2 * HD), 1)
            if first:
                state = jnp.where(lane == 2 * HD - 1, FAR, 0.0)
            else:
                state = state_ref[pl.ds(row, rows), :]
            for key in range(0, keys, tile):
                s = scores(qx[pl.ds(row, rows), :], kx[key : key + tile, :])
                old = state[:, 2 * HD - 1 :]
                top = jnp.maximum(old, jnp.max(s, axis=1, keepdims=True))
                weights = jnp.exp2(s - top).astype(bf16)
                update = product(weights, vx[key : key + tile, :], ((1,), (0,)))
                state = state * jnp.exp2(old - top) + update
                state = jnp.where(lane == 2 * HD - 1, top, state)
            put(row, state)
            return carry

        lax.fori_loop(0, STEP, head, 0)


def attend(first, last, place, docs, queries, kv, plain=None, norm=None, state=None):
    rows, width = queries.shape
    keys = kv.shape[0]
    heads = width // HD
    steps = heads // STEP
    smem = pl.BlockSpec(memory_space=pltpu.SMEM)
    whole = lambda shape: pl.BlockSpec(shape, lambda i: (0, 0))
    state_spec = pl.BlockSpec((STEP * rows, 2 * HD), lambda i: (i, 0))
    row_spec = pl.BlockSpec((rows, STEP * HD), lambda i: (0, i))
    in_specs = [smem] + ([] if first else [smem, smem])
    in_specs += [whole((2, HD)), row_spec, whole((keys, 2 * HD))] + ([] if first else [state_spec])
    args = [place] + ([] if first else [plain, norm]) + [docs, queries, kv] + ([] if first else [state])
    if last:
        out_shape = [jax.ShapeDtypeStruct(queries.shape, bf16)]
        out_specs = [row_spec]
    else:
        out_shape = [jax.ShapeDtypeStruct((heads * rows, 2 * HD), f32), jax.ShapeDtypeStruct((steps,), jnp.int32)]
        out_specs = [state_spec, smem]
    if first:
        out_shape.append(jax.ShapeDtypeStruct((steps,), f32))
        out_specs.append(smem)
    return pl.pallas_call(
        partial(kernel, first, last),
        out_shape=out_shape,
        grid=(steps,),
        in_specs=in_specs,
        out_specs=out_specs,
        scratch_shapes=[
            pltpu.VMEM((keys, 2 * HD), bf16),
            pltpu.VMEM((keys, 2 * HD), bf16),
            pltpu.VMEM((STEP * rows, 2 * HD), bf16),
            pltpu.SMEM((1,), f32),
        ],
        compiler_params=pltpu.CompilerParams(vmem_limit_bytes=40 * 2**20),
        cost_estimate=pl.CostEstimate(
            flops=8 * heads * rows * keys * HD,
            bytes_accessed=2 * rows * width + heads * rows * HD * 8,
            transcendentals=heads * rows * keys,
        ),
    )(*args)


def passed_along(x, by):
    count = lax.axis_size("qctx")
    return lax.ppermute(x, "qctx", [(i, i + by) for i in range(count - by)])


def shards(queries, keys, values, doc_lengths):
    rows = queries.shape[0]
    fine = lax.axis_size("kctx")
    block, part = lax.axis_index("qctx"), lax.axis_index("kctx")
    block_rows = fine * rows
    ends = jnp.cumsum(doc_lengths)
    docs = jnp.pad(jnp.stack([ends - doc_lengths, ends]), ((0, 0), (0, HD - ends.shape[0])))
    own_start = block * block_rows + part * rows

    def place(key_start, wrap_at):
        return jnp.stack([own_start, key_start, wrap_at, jnp.int32(block_rows)]).astype(jnp.int32)

    own = jnp.concatenate([keys, values], axis=1)
    one_back = passed_along(own, 1)
    two_back = passed_along(own, 2)
    later = jnp.arange(fine)[:, None, None] > part
    near = lax.all_to_all(jnp.where(later, own[None], one_back[None]), "kctx", 0, 0)
    far = lax.all_to_all(jnp.where(later, one_back[None], two_back[None]), "kctx", 0, 0)
    near, far = near.reshape(block_rows, 2 * HD), far.reshape(block_rows, 2 * HD)

    state, plain, norm = attend(True, False, place(own_start, rows), docs, queries, own)
    start = block * block_rows
    state, plain = attend(False, False, place(start, part * rows), docs, queries, near, plain, norm, state)
    return attend(False, True, place(start - block_rows, part * rows), docs, queries, far, plain, norm, state)[0]


def solution(mesh):
    placed = P(("qctx", "kctx"), "head")
    return jax.shard_map(
        shards, mesh=mesh, in_specs=(placed, placed, placed, P()), out_specs=placed, check_vma=False
    )
```

time: 156 us -> 111 us (0.71)
  the two profiles are of different devices: /device:TPU:248 before, /device:TPU:98 now
where the time goes in v1:
time: 111 us; the launch traced here: 110 us
  Pallas kernels  62.7 us (56%)
  starting transfers between devices  22.6 us (20%)
  waiting for transfers between devices  14.2 us (13%)
  local copies, waits for them, and re-layouts  8.83 us (8%)
  other arithmetic  1.73 us (2%)
    pallas_call x3, Pallas kernels, attend(): pl.pallas_call(partial(kernel, first, last), out_shape=out_shape, grid=(s...  62.7 us
    all_to_all x1, waiting for transfers between devices, shards(): lax.all_to_all(jnp.where(later, own[None], one_back[None]), 'kctx', 0, 0)  11.3 us
    ppermute x2, starting transfers between devices, passed_along(): return lax.ppermute(x, 'qctx', [(i, i + by) for i in range(count - by)])  10.2 us
    unnamed x13, local copies, waits for them, and re-layouts  7.93 us
    all_to_all x1, starting transfers between devices, shards(): lax.all_to_all(jnp.where(later, own[None], one_back[None]), 'kctx', 0, 0)  7.46 us
    all_to_all x1, starting transfers between devices, shards(): lax.all_to_all(jnp.where(later, one_back[None], two_back[None]), 'kctx',...  4.9 us
    ppermute x2, waiting for transfers between devices, passed_along(): return lax.ppermute(x, 'qctx', [(i, i + by) for i in range(count - by)])  2.91 us
  transfers between devices with their start and end apart: 4, of which 3 were waited for; matrix products, arithmetic and copies ran while one was open for 0% of the time, Pallas kernels for 33%

profile of v1, /device:TPU:98, one launch (start us, length us, event | category | flops | bytes accessed | tf_op | source)
XLA Modules:
  0.0 110.1 jit_solution(17593319988523984454)
XLA Ops:
  0.0 0.0 copy-start.5
  0.0 0.0 copy-start
  0.0 0.9 constant_dynamic-update-slice_fusion.1
  0.9 0.8 constant_dynamic-update-slice_fusion.refs_3_
  1.7 6.4 %collective-permute-start.1 = (bf16[192,256]{1,0:T(8,128)(2,1)S(1)}, bf16[192,256]{1,0:T(8,128)(2,1)S(1)}, u32[]{:S(2)}, u32[]{:S(2)}) collective-permute-start(bf16[192,256]{1,0:T(8,128)(2,1)S(1)} %constant_dynamic-update-slice_fusion.refs_3_), channel_id=1, source_target_pairs={{0,16},{8,24},{16,32},{24,40},{32,48},{40,56},{48,64},{56,72},{64,... | collective-permute-start | bytes 294920 | tf_op jit(solution)/shard_map/ppermute | solution.py:176
  8.1 3.8 %collective-permute-start = (bf16[192,256]{1,0:T(8,128)(2,1)S(1)}, bf16[192,256]{1,0:T(8,128)(2,1)S(1)}, u32[]{:S(2)}, u32[]{:S(2)}) collective-permute-start(bf16[192,256]{1,0:T(8,128)(2,1)S(1)} %constant_dynamic-update-slice_fusion.refs_3_), channel_id=1, source_target_pairs={{0,8},{8,16},{16,24},{24,32},{32,40},{40,48},{48,56},{56,64},{64,7... | collective-permute-start | bytes 294920 | tf_op jit(solution)/shard_map/ppermute | solution.py:176
  12.0 0.3 collective-permute-done.1
  12.3 2.6 %collective-permute-done = bf16[192,256]{1,0:T(8,128)(2,1)S(1)} collective-permute-done((bf16[192,256]{1,0:T(8,128)(2,1)S(1)}, bf16[192,256]{1,0:T(8,128)(2,1)S(1)}, u32[]{:S(2)}, u32[]{:S(2)}) %collective-permute-start) | collective-permute-done | bytes 98336 | tf_op jit(solution)/shard_map/ppermute | solution.py:176
  14.9 1.3 %broadcast_select_fusion = (bf16[8,192,256]{2,1,0:T(8,128)(2,1)}, bf16[8,192,256]{2,1,0:T(8,128)(2,1)}) fusion(pred[8]{0:T(512)(128)(4,1)S(1)} %iota_compare_fusion, bf16[192,256]{1,0:T(8,128)(2,1)S(1)} %collective-permute-done.1, bf16[192,256]{1,0:T(8,128)(2,1)S(1)} %collective-permute-done, bf16[192,256]{1,0:T(8,128)(2,1)S(1)} %constant_dynamic-update-slice_fusion.refs_3_), kind=kLoop, calls=%fused_computation | loop fusion | flops 786432 | bytes 1867784 | tf_op jit(solution)/shard_map/jit(_where)/select_n | solution.py:196
  16.2 7.5 %all-to-all-start = ((bf16[8,192,256]{2,1,0:T(8,128)(2,1)}), bf16[8,192,256]{2,1,0:T(8,128)(2,1)S(1)}, u32[]{:S(2)}, u32[]{:S(2)}) async-start(bf16[8,192,256]{2,1,0:T(8,128)(2,1)} %get-tuple-element.16), calls=%async_computation | async-start | bytes 1572864 | tf_op jit(solution)/shard_map/all_to_all | solution.py:195
  23.6 0.0 copy-done.5
  23.7 0.1 copy.6
  23.8 0.1 reduce
  23.9 0.1 pad_add_fusion.1.refs_0_
  24.0 11.3 %all-to-all-done = bf16[8,192,256]{2,1,0:T(8,128)(2,1)S(1)} async-done(((bf16[8,192,256]{2,1,0:T(8,128)(2,1)}), bf16[8,192,256]{2,1,0:T(8,128)(2,1)S(1)}, u32[]{:S(2)}, u32[]{:S(2)}) %all-to-all-start) | async-done | bytes 786464 | tf_op jit(solution)/shard_map/all_to_all | solution.py:195
  35.3 4.9 %all-to-all-start.1 = ((bf16[8,192,256]{2,1,0:T(8,128)(2,1)}), bf16[8,192,256]{2,1,0:T(8,128)(2,1)S(1)}, u32[]{:S(2)}, u32[]{:S(2)}) async-start(bf16[8,192,256]{2,1,0:T(8,128)(2,1)} %get-tuple-element.15), calls=%async_computation.1 | async-start | bytes 1572864 | tf_op jit(solution)/shard_map/all_to_all | solution.py:196
  40.2 0.0 copy-done
  40.2 11.7 %shard_map.46 = (f32[3072,256]{1,0:T(8,128)S(1)}, s32[4]{0:T(128)S(1)}, f32[4]{0:T(128)S(1)}) custom-call(s32[4]{0:T(128)S(1)} %pad_add_fusion.1.refs_0_, s32[2,128]{1,0:T(2,128)S(1)} %pad.4.refs_1_.refs_3_, bf16[192,2048]{1,0:T(8,128)(2,1)S(1)} %copy-done, bf16[192,256]{1,0:T(8,128)(2,1)S(1)} %constant_dynamic-update-slice_fusion.refs_3_), custom_call_target="tpu_custom_call" | custom-call | flops 603979776 | bytes 3932160 | tf_op jit(solution)/shard_map/pallas_call | solution.py:153
  51.9 0.0 copy-start.1
  51.9 1.6 %copy-done.1 = f32[3072,256]{1,0:T(8,128)} copy-done((f32[3072,256]{1,0:T(8,128)}, f32[3072,256]{1,0:T(8,128)S(1)}, u32[]{:S(2)}) %copy-start.1) | copy-done | bytes 3145752
  53.5 0.1 pad_add_fusion.2.refs_0_
  53.6 0.1 pad_add_fusion.3.refs_0_
  53.7 0.0 copy-start.2
  53.7 1.9 %copy-done.2 = f32[3072,256]{1,0:T(8,128)S(1)} copy-done((f32[3072,256]{1,0:T(8,128)S(1)}, f32[3072,256]{1,0:T(8,128)}, u32[]{:S(2)}) %copy-start.2) | copy-done | bytes 3145752
  55.6 24.9 %shard_map.47 = (f32[3072,256]{1,0:T(8,128)S(1)}, s32[4]{0:T(128)S(1)}) custom-call(s32[4]{0:T(128)S(1)} %pad_add_fusion.2.refs_0_, s32[4]{0:T(128)S(1)} %get-tuple-element.10.refs_1_, f32[4]{0:T(128)S(1)} %get-tuple-element.11.refs_2_, s32[2,128]{1,0:T(2,128)S(1)} %pad.4.refs_1_.refs_3_, bf16[192,2048]{1,0:T(8,128)(2,1)S(1)} %copy-done, ...), custom_call_target="tpu_custom_call" | custom-call | flops 4831838208 | bytes 3932160 | tf_op jit(solution)/shard_map/pallas_call | solution.py:153
  80.5 0.0 copy-start.3
  80.5 1.6 %copy-done.3 = f32[3072,256]{1,0:T(8,128)} copy-done((f32[3072,256]{1,0:T(8,128)}, f32[3072,256]{1,0:T(8,128)S(1)}, u32[]{:S(2)}) %copy-start.3) | copy-done | bytes 3145752
  82.1 0.0 all-to-all-done.1
  82.2 0.0 copy-start.4
  82.2 1.9 %copy-done.4 = f32[3072,256]{1,0:T(8,128)S(1)} copy-done((f32[3072,256]{1,0:T(8,128)S(1)}, f32[3072,256]{1,0:T(8,128)}, u32[]{:S(2)}) %copy-start.4) | copy-done | bytes 3145752
  84.0 26.1 %shard_map.48 = bf16[192,2048]{1,0:T(8,128)(2,1)} custom-call(s32[4]{0:T(128)S(1)} %pad_add_fusion.3.refs_0_, s32[4]{0:T(128)S(1)} %get-tuple-element.13.refs_1_, f32[4]{0:T(128)S(1)} %get-tuple-element.11.refs_2_, s32[2,128]{1,0:T(2,128)S(1)} %pad.4.refs_1_.refs_3_, bf16[192,2048]{1,0:T(8,128)(2,1)S(1)} %copy-done, bf16[1536,256]{1,0:T(8,128)(2,1)S(1)} %bitcast.11, ...), custom_call_target="tpu_custom_call" | custom-call | flops 4831838208 | bytes 3932160 | tf_op jit(solution)/shard_map/pallas_call | solution.py:153
  (5 shorter events, 0.1 us)
Async XLA Ops:
  0.0 23.6 %copy-start.5 = (s32[16]{0:T(128)S(1)}, s32[16]{0:T(128)}, u32[]{:S(2)}) copy-start(s32[16]{0:T(128)} %param.7) | copy-start | bytes 196
  0.0 40.2 %copy-start = (bf16[192,2048]{1,0:T(8,128)(2,1)S(1)}, bf16[192,2048]{1,0:T(8,128)(2,1)}, u32[]{:S(2)}) copy-start(bf16[192,2048]{1,0:T(8,128)(2,1)} %refs_4_.3) | copy-start | bytes 2359300
  1.7 10.6 %collective-permute-start.1 = (bf16[192,256]{1,0:T(8,128)(2,1)S(1)}, bf16[192,256]{1,0:T(8,128)(2,1)S(1)}, u32[]{:S(2)}, u32[]{:S(2)}) collective-permute-start(bf16[192,256]{1,0:T(8,128)(2,1)S(1)} %constant_dynamic-update-slice_fusion.refs_3_), channel_id=1, source_target_pairs={{0,16},{8,24},{16,32},{24,40},{32,48},{40,56},{48,64},{56,72},{64,... | collective-permute-start | bytes 294920 | tf_op jit(solution)/shard_map/ppermute | solution.py:176
  8.1 6.8 %collective-permute-start = (bf16[192,256]{1,0:T(8,128)(2,1)S(1)}, bf16[192,256]{1,0:T(8,128)(2,1)S(1)}, u32[]{:S(2)}, u32[]{:S(2)}) collective-permute-start(bf16[192,256]{1,0:T(8,128)(2,1)S(1)} %constant_dynamic-update-slice_fusion.refs_3_), channel_id=1, source_target_pairs={{0,8},{8,16},{16,24},{24,32},{32,40},{40,48},{48,56},{56,64},{64,7... | collective-permute-start | bytes 294920 | tf_op jit(solution)/shard_map/ppermute | solution.py:176
  16.2 19.1 %all-to-all-start = ((bf16[8,192,256]{2,1,0:T(8,128)(2,1)}), bf16[8,192,256]{2,1,0:T(8,128)(2,1)S(1)}, u32[]{:S(2)}, u32[]{:S(2)}) async-start(bf16[8,192,256]{2,1,0:T(8,128)(2,1)} %get-tuple-element.16), calls=%async_computation | async-start | bytes 1572864 | tf_op jit(solution)/shard_map/all_to_all | solution.py:195
  35.3 46.8 %all-to-all-start.1 = ((bf16[8,192,256]{2,1,0:T(8,128)(2,1)}), bf16[8,192,256]{2,1,0:T(8,128)(2,1)S(1)}, u32[]{:S(2)}, u32[]{:S(2)}) async-start(bf16[8,192,256]{2,1,0:T(8,128)(2,1)} %get-tuple-element.15), calls=%async_computation.1 | async-start | bytes 1572864 | tf_op jit(solution)/shard_map/all_to_all | solution.py:196
  51.9 1.6 %copy-start.1 = (f32[3072,256]{1,0:T(8,128)}, f32[3072,256]{1,0:T(8,128)S(1)}, u32[]{:S(2)}) copy-start(f32[3072,256]{1,0:T(8,128)S(1)} %get-tuple-element.12.refs_6_) | copy-start | bytes 9437188
  53.7 1.9 %copy-start.2 = (f32[3072,256]{1,0:T(8,128)S(1)}, f32[3072,256]{1,0:T(8,128)}, u32[]{:S(2)}) copy-start(f32[3072,256]{1,0:T(8,128)} %copy-done.1) | copy-start | bytes 9437188
  80.5 1.6 %copy-start.3 = (f32[3072,256]{1,0:T(8,128)}, f32[3072,256]{1,0:T(8,128)S(1)}, u32[]{:S(2)}) copy-start(f32[3072,256]{1,0:T(8,128)S(1)} %get-tuple-element.14.refs_6_) | copy-start | bytes 9437188
  82.2 1.9 %copy-start.4 = (f32[3072,256]{1,0:T(8,128)S(1)}, f32[3072,256]{1,0:T(8,128)}, u32[]{:S(2)}) copy-start(f32[3072,256]{1,0:T(8,128)} %copy-done.3) | copy-start | bytes 9437188

commit v2 on v1

v2 whole, which is shorter than its diff:
```python
from functools import partial

import jax
import jax.numpy as jnp
from jax import lax
from jax.experimental import pallas as pl
from jax.experimental.pallas import tpu as pltpu
from jax.sharding import PartitionSpec as P

HD = 128
SUB = 2
LEAN_TILE = 512
VMEM_BYTES = 50 * 2**20
PARTS = 2
TILE = 512
SCALE = HD**-0.5 * 1.4426950408889634
SAFE = 100.0
FAR = -(2.0**100)

bf16 = jnp.bfloat16
f32 = jnp.float32


def product(a, b, dims):
    return lax.dot_general(a, b, (dims, ((), ())), preferred_element_type=f32)


def largest_norm(x):
    squares = (x.astype(f32) * x.astype(f32)).astype(bf16)
    sums = product(squares, jnp.ones((HD, HD), bf16), ((1,), (0,)))
    return jnp.max(sums) * 1.02


def kernel(first, back, *refs):
    if first:
        lengths, q_ref, kv_ref, own_ref, out_hbm, guard_out, *scratch = refs
    else:
        lengths, guard_in, q_ref, kv_ref, state_hbm, out_hbm, *scratch = refs
    state_ref, out_ref, kx, vx, sems = scratch
    keys = kv_ref.shape[0]
    rows, width = q_ref.shape
    heads = width // HD
    size = SUB * rows
    every = keys + rows if first else keys
    block, part = lax.axis_index("qctx"), lax.axis_index("kctx")

    def copy_out(i):
        if first:
            here = pl.ds(i * (heads // PARTS) * rows, heads // PARTS * rows)
            return pltpu.make_async_copy(state_ref.at[here], out_hbm.at[here], sems.at[i])
        here = pl.ds(i * (width // PARTS), width // PARTS)
        return pltpu.make_async_copy(out_ref.at[:, here], out_hbm.at[:, here], sems.at[i])

    if not first:
        get_state = pltpu.make_async_copy(state_hbm, state_ref, sems.at[PARTS])
        get_state.start()

    lane = lax.broadcasted_iota(jnp.int32, (1, HD), 1)
    starts = jnp.zeros((1, HD), jnp.int32)
    ends = jnp.zeros((1, HD), jnp.int32)
    run = jnp.int32(0)
    for d in range(lengths.shape[0]):
        starts = jnp.where(lane == d, run, starts)
        run = run + lengths[d]
        ends = jnp.where(lane == d, run, ends)
    at = lax.broadcasted_iota(jnp.int32, (keys, HD), 0)
    pos = block * keys + at - jnp.where(at >= part * rows, keys, 0) - back * keys
    kx[0:keys, HD:] = jnp.where((pos >= starts) & (pos < ends), 0.0, FAR).astype(bf16)
    at = lax.broadcasted_iota(jnp.int32, (rows, HD), 0) + block * keys + part * rows
    mine = (at >= starts) & (at < ends)
    onehot = jnp.where(mine, 1.0, 0.0).astype(bf16)
    vx[:, HD:] = jnp.ones((every, HD), bf16)
    kx[0:keys, 0:HD] = kv_ref[:, 0:HD]
    vx[0:keys, 0:HD] = kv_ref[:, HD:]
    knorm = largest_norm(kv_ref[:, 0:HD])
    if first:
        kx[keys:, HD:] = jnp.where(mine, 0.0, FAR).astype(bf16)
        kx[keys:, 0:HD] = own_ref[:, 0:HD]
        vx[keys:, 0:HD] = own_ref[:, HD:]
        knorm = jnp.maximum(knorm, largest_norm(own_ref[:, 0:HD]))
        qnorm = largest_norm(q_ref[:, 0:HD])
        for h in range(1, heads):
            qnorm = jnp.maximum(qnorm, largest_norm(q_ref[:, h * HD : (h + 1) * HD]))
    else:
        qnorm = guard_in[1]
    plain = qnorm * knorm <= (SAFE / SCALE) ** 2
    if first:
        guard_out[0] = plain.astype(f32)
        guard_out[1] = qnorm
    else:
        plain = plain & (guard_in[0] == 1.0)
        get_state.wait()

    def scores(q, key, count):
        s = product(q, kx[key : key + count, :], ((1,), (1,))) * SCALE
        if key == keys:
            r = lax.broadcasted_iota(jnp.int32, (rows, rows), 0)
            c = lax.broadcasted_iota(jnp.int32, (rows, rows), 1)
            s = jnp.where(jnp.concatenate([c <= r] * (q.shape[0] // rows), axis=0), s, FAR)
        return s

    def tiles(tile):
        return [(key, tile) for key in range(0, keys, tile)] + ([(keys, rows)] if first else [])

    def divided(part):
        total = jnp.broadcast_to(part[:, HD : HD + 1], (rows, HD))
        return (part[:, 0:HD] / total).astype(bf16)

    @pl.when(plain)
    def _():
        for i in range(PARTS):
            for head in range(i * heads // PARTS, (i + 1) * heads // PARTS, SUB):
                here = slice(head * rows, head * rows + size)
                group = range(head, head + SUB)
                q = [jnp.concatenate([q_ref[:, h * HD : (h + 1) * HD], onehot], axis=1) for h in group]
                q = jnp.concatenate(q, axis=0)
                state = None if first else state_ref[here, :]
                for key, count in tiles(TILE):
                    weights = jnp.exp2(scores(q, key, count)).astype(bf16)
                    update = product(weights, vx[key : key + count, :], ((1,), (0,)))
                    state = update if state is None else state + update
                if first:
                    lanes = lax.broadcasted_iota(jnp.int32, state.shape, 1)
                    state_ref[here, :] = jnp.where(lanes == 2 * HD - 1, 0.0, state)
                else:
                    for n, h in enumerate(group):
                        out_ref[:, h * HD : (h + 1) * HD] = divided(state[n * rows : (n + 1) * rows])
            copy_out(i).start()

    @pl.when(jnp.logical_not(plain))
    def _():
        def one(head, carry):
            row = pl.multiple_of(head * rows, rows)
            column = pl.multiple_of(head * HD, HD)
            lanes = lax.broadcasted_iota(jnp.int32, (rows, 2 * HD), 1)
            if first:
                state = jnp.where(lanes == 2 * HD - 1, FAR, 0.0)
            else:
                state = state_ref[pl.ds(row, rows), :]
            q = jnp.concatenate([q_ref[:, pl.ds(column, HD)], onehot], axis=1)
            for key, count in reversed(tiles(LEAN_TILE)):
                s = scores(q, key, count)
                old = state[:, 2 * HD - 1 :]
                top = jnp.maximum(old, jnp.max(s, axis=1, keepdims=True))
                weights = jnp.exp2(s - top).astype(bf16)
                update = product(weights, vx[key : key + count, :], ((1,), (0,)))
                state = state * jnp.exp2(old - top) + update
                state = jnp.where(lanes == 2 * HD - 1, top, state)
            if first:
                state_ref[pl.ds(row, rows), :] = state
            else:
                out_ref[:, pl.ds(column, HD)] = divided(state)
            return carry

        lax.fori_loop(0, heads, one, 0)
        for i in range(PARTS):
            copy_out(i).start()

    for i in range(PARTS):
        copy_out(i).wait()


def attend(first, back, doc_lengths, queries, kv, *rest):
    rows, width = queries.shape
    keys = kv.shape[0]
    every = keys + rows if first else keys
    heads = width // HD
    smem = pl.BlockSpec(memory_space=pltpu.SMEM)
    vmem = pl.BlockSpec(memory_space=pltpu.VMEM)
    hbm = pl.BlockSpec(memory_space=pltpu.HBM)
    if first:
        args = (doc_lengths, queries, kv) + rest
        in_specs = [smem, vmem, vmem, vmem]
        out_shape = [jax.ShapeDtypeStruct((heads * rows, 2 * HD), f32), jax.ShapeDtypeStruct((2,), f32)]
        out_specs = [hbm, smem]
    else:
        state, guard = rest
        args = (doc_lengths, guard, queries, kv, state)
        in_specs = [smem, smem, vmem, vmem, hbm]
        out_shape = jax.ShapeDtypeStruct(queries.shape, bf16)
        out_specs = hbm
    return pl.pallas_call(
        partial(kernel, first, back),
        out_shape=out_shape,
        in_specs=in_specs,
        out_specs=out_specs,
        scratch_shapes=[
            pltpu.VMEM((heads * rows, 2 * HD), f32),
            pltpu.VMEM((8, HD) if first else (rows, width), bf16),
            pltpu.VMEM((every, 2 * HD), bf16),
            pltpu.VMEM((every, 2 * HD), bf16),
            pltpu.SemaphoreType.DMA((PARTS + 1,)),
        ],
        compiler_params=pltpu.CompilerParams(vmem_limit_bytes=VMEM_BYTES),
        cost_estimate=pl.CostEstimate(
            flops=8 * heads * rows * every * HD,
            bytes_accessed=2 * rows * width + heads * rows * HD * 8,
            transcendentals=heads * rows * every,
        ),
    )(*args)


def passed_along(x, by):
    count = lax.axis_size("qctx")
    return lax.ppermute(x, "qctx", [(i, i + by) for i in range(count - by)])


def to_parts(upward, downward):
    fine = lax.axis_size("kctx")
    later = jnp.arange(fine)[:, None, None] > lax.axis_index("kctx")
    return jnp.where(later, upward[None], downward[None])


def beside(keys, values):
    low = jnp.array(-jnp.inf, bf16)
    keys = lax.pad(keys, low, ((0, 0, 0), (0, HD, 0)))
    return jnp.maximum(keys, lax.pad(values, low, ((0, 0, 0), (HD, 0, 0))))


def shards(queries, keys, values, doc_lengths):
    block_rows = lax.axis_size("kctx") * queries.shape[0]
    own = beside(keys, values)
    one_back = passed_along(own, 1)
    near_parts, held = lax.optimization_barrier((to_parts(own, one_back), one_back))
    near = lax.all_to_all(near_parts, "kctx", 0, 0).reshape(block_rows, 2 * HD)
    two_back = passed_along(held, 1)
    far = lax.all_to_all(to_parts(held, two_back), "kctx", 0, 0).reshape(block_rows, 2 * HD)
    carried = attend(True, 0, doc_lengths, queries, near, own)
    return attend(False, 1, doc_lengths, queries, far, *carried)


def solution(mesh):
    placed = P(("qctx", "kctx"), "head")
    return jax.shard_map(
        shards, mesh=mesh, in_specs=(placed, placed, placed, P()), out_specs=placed, check_vma=False
    )
```

time: 111 us -> 91.6 us (0.83)
  the two profiles are of different devices: /device:TPU:98 before, /device:TPU:258 now
where the time goes in v2:
time: 91.6 us; the launch traced here: 91.3 us
  Pallas kernels  57.9 us (63%)
  starting transfers between devices  17.2 us (19%)
  waiting for transfers between devices  13 us (14%)
  other arithmetic  2.93 us (3%)
    pallas_call x2, Pallas kernels, attend(): pl.pallas_call(partial(kernel, first, back), out_shape=out_shape, in_spec...  57.9 us
    ppermute x2, waiting for transfers between devices, passed_along(): return lax.ppermute(x, 'qctx', [(i, i + by) for i in range(count - by)])  10.6 us
    all_to_all x1, starting transfers between devices, shards(): near = lax.all_to_all(near_parts, 'kctx', 0, 0).reshape(block_rows, 2 * HD)  7.46 us
    all_to_all x1, starting transfers between devices, shards(): lax.all_to_all(to_parts(held, two_back), 'kctx', 0, 0)  4.93 us
    ppermute x2, starting transfers between devices, passed_along(): return lax.ppermute(x, 'qctx', [(i, i + by) for i in range(count - by)])  4.84 us
    all_to_all x1, waiting for transfers between devices, shards(): near = lax.all_to_all(near_parts, 'kctx', 0, 0).reshape(block_rows, 2 * HD)  2.41 us
    select_n x2, other arithmetic, to_parts(): return jnp.where(later, upward[None], downward[None])  2.01 us
  transfers between devices with their start and end apart: 4, of which 3 were waited for; matrix products, arithmetic and copies ran while one was open for 1% of the time, Pallas kernels for 34%

profile of v2, /device:TPU:258, one launch (start us, length us, event | category | flops | bytes accessed | tf_op | source)
XLA Modules:
  0.0 91.3 jit_solution(13345091494013532443)
XLA Ops:
  0.0 0.0 copy-start.1
  0.0 0.0 copy-start
  0.0 0.9 pad_maximum_fusion.refs_3_
  0.9 2.9 %collective-permute-start = (bf16[192,256]{1,0:T(8,128)(2,1)S(1)}, bf16[192,256]{1,0:T(8,128)(2,1)S(1)}, u32[]{:S(2)}, u32[]{:S(2)}) collective-permute-start(bf16[192,256]{1,0:T(8,128)(2,1)S(1)} %pad_maximum_fusion.refs_3_), channel_id=1, source_target_pairs={{0,8},{8,16},{16,24},{24,32},{32,40},{40,48},{48,56},{56,64},{64,7... | collective-permute-start | bytes 294920 | tf_op jit(solution)/shard_map/ppermute | solution.py:205
  3.9 4.8 %collective-permute-done = bf16[192,256]{1,0:T(8,128)(2,1)S(1)} collective-permute-done((bf16[192,256]{1,0:T(8,128)(2,1)S(1)}, bf16[192,256]{1,0:T(8,128)(2,1)S(1)}, u32[]{:S(2)}, u32[]{:S(2)}) %collective-permute-start) | collective-permute-done | bytes 98336 | tf_op jit(solution)/shard_map/ppermute | solution.py:205
  8.6 1.0 %broadcast_select_fusion.1 = bf16[8,192,256]{2,1,0:T(8,128)(2,1)} fusion(pred[8]{0:T(512)(128)(4,1)S(1)} %iota_compare_fusion, bf16[192,256]{1,0:T(8,128)(2,1)S(1)} %collective-permute-done, bf16[192,256]{1,0:T(8,128)(2,1)S(1)} %pad_maximum_fusion.refs_3_), kind=kLoop, calls=%fused_computation.1 | loop fusion | flops 393216 | bytes 983048 | tf_op jit(solution)/shard_map/jit(_where)/select_n | solution.py:211
  9.6 7.5 %all-to-all-start = ((bf16[8,192,256]{2,1,0:T(8,128)(2,1)}), bf16[8,192,256]{2,1,0:T(8,128)(2,1)S(1)}, u32[]{:S(2)}, u32[]{:S(2)}) async-start(bf16[8,192,256]{2,1,0:T(8,128)(2,1)} %broadcast_select_fusion.1), calls=%async_computation | async-start | bytes 1572864 | tf_op jit(solution)/shard_map/all_to_all | solution.py:225
  17.1 1.9 %collective-permute-start.1 = (bf16[192,256]{1,0:T(8,128)(2,1)S(1)}, bf16[192,256]{1,0:T(8,128)(2,1)S(1)}, u32[]{:S(2)}, u32[]{:S(2)}) collective-permute-start(bf16[192,256]{1,0:T(8,128)(2,1)S(1)} %collective-permute-done), channel_id=1, source_target_pairs={{0,8},{8,16},{16,24},{24,32},{32,40},{40,48},{48,56},{56,64},{64,7... | collective-permute-start | bytes 294920 | tf_op jit(solution)/shard_map/ppermute | solution.py:205
  19.0 5.8 %collective-permute-done.1 = bf16[192,256]{1,0:T(8,128)(2,1)S(1)} collective-permute-done((bf16[192,256]{1,0:T(8,128)(2,1)S(1)}, bf16[192,256]{1,0:T(8,128)(2,1)S(1)}, u32[]{:S(2)}, u32[]{:S(2)}) %collective-permute-start.1) | collective-permute-done | bytes 98336 | tf_op jit(solution)/shard_map/ppermute | solution.py:205
  24.8 1.0 %broadcast_select_fusion = bf16[8,192,256]{2,1,0:T(8,128)(2,1)} fusion(pred[8]{0:T(512)(128)(4,1)S(1)} %iota_compare_fusion, bf16[192,256]{1,0:T(8,128)(2,1)S(1)} %collective-permute-done.1, bf16[192,256]{1,0:T(8,128)(2,1)S(1)} %collective-permute-done), kind=kLoop, calls=%fused_computation | loop fusion | flops 393216 | bytes 983048 | tf_op jit(solution)/shard_map/jit(_where)/select_n | solution.py:211
  25.8 2.4 %all-to-all-done = bf16[8,192,256]{2,1,0:T(8,128)(2,1)S(1)} async-done(((bf16[8,192,256]{2,1,0:T(8,128)(2,1)}), bf16[8,192,256]{2,1,0:T(8,128)(2,1)S(1)}, u32[]{:S(2)}, u32[]{:S(2)}) %all-to-all-start) | async-done | bytes 786464 | tf_op jit(solution)/shard_map/all_to_all | solution.py:225
  28.2 4.9 %all-to-all-start.1 = ((bf16[8,192,256]{2,1,0:T(8,128)(2,1)}), bf16[8,192,256]{2,1,0:T(8,128)(2,1)S(1)}, u32[]{:S(2)}, u32[]{:S(2)}) async-start(bf16[8,192,256]{2,1,0:T(8,128)(2,1)} %broadcast_select_fusion), calls=%async_computation.1 | async-start | bytes 1572864 | tf_op jit(solution)/shard_map/all_to_all | solution.py:227
  33.2 0.0 copy-done.1
  33.2 0.0 copy-done
  33.2 30.8 %shard_map.46 = (f32[3072,256]{1,0:T(8,128)}, f32[2]{0:T(128)S(1)}) custom-call(s32[16]{0:T(128)S(1)} %copy-done.1, bf16[192,2048]{1,0:T(8,128)(2,1)S(1)} %copy-done, bf16[1536,256]{1,0:T(8,128)(2,1)S(1)} %bitcast.2, bf16[192,256]{1,0:T(8,128)(2,1)S(1)} %pad_maximum_fusion.refs_3_), custom_call_target="tpu_custom_call" | custom-call | flops 5435817984 | bytes 3932160 | tf_op jit(solution)/shard_map/pallas_call | solution.py:182
  64.0 0.0 all-to-all-done.1
  64.0 27.1 %shard_map.47 = bf16[192,2048]{1,0:T(8,128)(2,1)} custom-call(s32[16]{0:T(128)S(1)} %copy-done.1, f32[2]{0:T(128)S(1)} %get-tuple-element.10.refs_1_, bf16[192,2048]{1,0:T(8,128)(2,1)S(1)} %copy-done, bf16[1536,256]{1,0:T(8,128)(2,1)S(1)} %bitcast.3, f32[3072,256]{1,0:T(8,128)} %get-tuple-element.12.refs_4_), custom_call_target="tpu_custom_call" | custom-call | flops 4831838208 | bytes 3932160 | tf_op jit(solution)/shard_map/pallas_call | solution.py:182
  (1 shorter events, 0.0 us)
Async XLA Ops:
  0.0 33.2 %copy-start.1 = (s32[16]{0:T(128)S(1)}, s32[16]{0:T(128)}, u32[]{:S(2)}) copy-start(s32[16]{0:T(128)} %refs_0_.3) | copy-start | bytes 196
  0.0 33.2 %copy-start = (bf16[192,2048]{1,0:T(8,128)(2,1)S(1)}, bf16[192,2048]{1,0:T(8,128)(2,1)}, u32[]{:S(2)}) copy-start(bf16[192,2048]{1,0:T(8,128)(2,1)} %refs_2_.1) | copy-start | bytes 2359300
  0.9 7.7 %collective-permute-start = (bf16[192,256]{1,0:T(8,128)(2,1)S(1)}, bf16[192,256]{1,0:T(8,128)(2,1)S(1)}, u32[]{:S(2)}, u32[]{:S(2)}) collective-permute-start(bf16[192,256]{1,0:T(8,128)(2,1)S(1)} %pad_maximum_fusion.refs_3_), channel_id=1, source_target_pairs={{0,8},{8,16},{16,24},{24,32},{32,40},{40,48},{48,56},{56,64},{64,7... | collective-permute-start | bytes 294920 | tf_op jit(solution)/shard_map/ppermute | solution.py:205
  9.6 18.6 %all-to-all-start = ((bf16[8,192,256]{2,1,0:T(8,128)(2,1)}), bf16[8,192,256]{2,1,0:T(8,128)(2,1)S(1)}, u32[]{:S(2)}, u32[]{:S(2)}) async-start(bf16[8,192,256]{2,1,0:T(8,128)(2,1)} %broadcast_select_fusion.1), calls=%async_computation | async-start | bytes 1572864 | tf_op jit(solution)/shard_map/all_to_all | solution.py:225
  17.1 7.7 %collective-permute-start.1 = (bf16[192,256]{1,0:T(8,128)(2,1)S(1)}, bf16[192,256]{1,0:T(8,128)(2,1)S(1)}, u32[]{:S(2)}, u32[]{:S(2)}) collective-permute-start(bf16[192,256]{1,0:T(8,128)(2,1)S(1)} %collective-permute-done), channel_id=1, source_target_pairs={{0,8},{8,16},{16,24},{24,32},{32,40},{40,48},{48,56},{56,64},{64,7... | collective-permute-start | bytes 294920 | tf_op jit(solution)/shard_map/ppermute | solution.py:205
  28.2 35.8 %all-to-all-start.1 = ((bf16[8,192,256]{2,1,0:T(8,128)(2,1)}), bf16[8,192,256]{2,1,0:T(8,128)(2,1)S(1)}, u32[]{:S(2)}, u32[]{:S(2)}) async-start(bf16[8,192,256]{2,1,0:T(8,128)(2,1)} %broadcast_select_fusion), calls=%async_computation.1 | async-start | bytes 1572864 | tf_op jit(solution)/shard_map/all_to_all | solution.py:227

commit v3 on v2

--- a/solution.py
+++ b/solution.py
@@ -72,6 +72,8 @@
     vx[:, HD:] = jnp.ones((every, HD), bf16)
     kx[0:keys, 0:HD] = kv_ref[:, 0:HD]
     vx[0:keys, 0:HD] = kv_ref[:, HD:]
+    if not first:
+        get_state.wait()
     knorm = largest_norm(kv_ref[:, 0:HD])
     if first:
         kx[keys:, HD:] = jnp.where(mine, 0.0, FAR).astype(bf16)
@@ -89,7 +91,6 @@
         guard_out[1] = qnorm
     else:
         plain = plain & (guard_in[0] == 1.0)
-        get_state.wait()
 
     def scores(q, key, count):
         s = product(q, kx[key : key + count, :], ((1,), (1,))) * SCALE
@@ -106,26 +107,26 @@
         total = jnp.broadcast_to(part[:, HD : HD + 1], (rows, HD))
         return (part[:, 0:HD] / total).astype(bf16)
 
-    @pl.when(plain)
-    def _():
-        for i in range(PARTS):
-            for head in range(i * heads // PARTS, (i + 1) * heads // PARTS, SUB):
-                here = slice(head * rows, head * rows + size)
-                group = range(head, head + SUB)
-                q = [jnp.concatenate([q_ref[:, h * HD : (h + 1) * HD], onehot], axis=1) for h in group]
-                q = jnp.concatenate(q, axis=0)
-                state = None if first else state_ref[here, :]
-                for key, count in tiles(TILE):
-                    weights = jnp.exp2(scores(q, key, count)).astype(bf16)
-                    update = product(weights, vx[key : key + count, :], ((1,), (0,)))
-                    state = update if state is None else state + update
-                if first:
-                    lanes = lax.broadcasted_iota(jnp.int32, state.shape, 1)
-                    state_ref[here, :] = jnp.where(lanes == 2 * HD - 1, 0.0, state)
-                else:
-                    for n, h in enumerate(group):
-                        out_ref[:, h * HD : (h + 1) * HD] = divided(state[n * rows : (n + 1) * rows])
-            copy_out(i).start()
+    for i in range(PARTS):
+        for head in range(i * heads // PARTS, (i + 1) * heads // PARTS, SUB):
+            here = slice(head * rows, head * rows + size)
+            group = range(head, head + SUB)
+            q = [jnp.concatenate([q_ref[:, h * HD : (h + 1) * HD], onehot], axis=1) for h in group]
+            q = jnp.concatenate(q, axis=0)
+            state = None if first else state_ref[here, :]
+            for key, count in tiles(TILE):
+                weights = jnp.exp2(scores(q, key, count)).astype(bf16)
+                update = product(weights, vx[key : key + count, :], ((1,), (0,)))
+                state = update if state is None else state + update
+            if first:
+                lanes = lax.broadcasted_iota(jnp.int32, state.shape, 1)
+                state_ref[here, :] = jnp.where(lanes == 2 * HD - 1, 0.0, state)
+            else:
+                for n, h in enumerate(group):
+                    out_ref[:, h * HD : (h + 1) * HD] = divided(state[n * rows : (n + 1) * rows])
+        copy_out(i).start()
+    for i in range(PARTS):
+        copy_out(i).wait()
 
     @pl.when(jnp.logical_not(plain))
     def _():
@@ -155,9 +156,8 @@
         lax.fori_loop(0, heads, one, 0)
         for i in range(PARTS):
             copy_out(i).start()
-
-    for i in range(PARTS):
-        copy_out(i).wait()
+        for i in range(PARTS):
+            copy_out(i).wait()
 
 
 def attend(first, back, doc_lengths, queries, kv, *rest):

time: 91.6 us -> 104 us (1.14)
  Pallas kernels: 57.9 us -> 70.3 us
    pallas_call x2, Pallas kernels: 57.9 us -> 70.3 us  [attend(): pl.pallas_call(partial(kernel, first, back), out_shape=out_shape, in_spec...]
  transfers between devices with their start and end apart: 4 -> 4, of which waited for: 3 -> 3; matrix products, arithmetic and copies ran while one was open for 1% -> 1% of each run, Pallas kernels for 34% -> 36%
where the time goes in v3:
time: 104 us
  Pallas kernels  70.3 us (68%)
  starting transfers between devices  17.2 us (17%)
  waiting for transfers between devices  13 us (12%)
  other arithmetic  2.93 us (3%)
    pallas_call x2, Pallas kernels, attend(): pl.pallas_call(partial(kernel, first, back), out_shape=out_shape, in_spec...  70.3 us
    ppermute x2, waiting for transfers between devices, passed_along(): return lax.ppermute(x, 'qctx', [(i, i + by) for i in range(count - by)])  10.6 us
    all_to_all x1, starting transfers between devices, shards(): near = lax.all_to_all(near_parts, 'kctx', 0, 0).reshape(block_rows, 2 * HD)  7.46 us
    all_to_all x1, starting transfers between devices, shards(): lax.all_to_all(to_parts(held, two_back), 'kctx', 0, 0)  4.93 us
    ppermute x2, starting transfers between devices, passed_along(): return lax.ppermute(x, 'qctx', [(i, i + by) for i in range(count - by)])  4.84 us
    all_to_all x1, waiting for transfers between devices, shards(): near = lax.all_to_all(near_parts, 'kctx', 0, 0).reshape(block_rows, 2 * HD)  2.41 us
  transfers between devices with their start and end apart: 4, of which 3 were waited for; matrix products, arithmetic and copies ran while one was open for 1% of the time, Pallas kernels for 36%

profile of v3, /device:TPU:258, one launch (start us, length us, event | category | flops | bytes accessed | tf_op | source)
XLA Modules:
  0.0 103.6 jit_solution(916500903406894591)
XLA Ops:
  0.0 0.0 copy-start.1
  0.0 0.0 copy-start
  0.0 0.9 pad_maximum_fusion.refs_3_
  0.9 2.9 %collective-permute-start = (bf16[192,256]{1,0:T(8,128)(2,1)S(1)}, bf16[192,256]{1,0:T(8,128)(2,1)S(1)}, u32[]{:S(2)}, u32[]{:S(2)}) collective-permute-start(bf16[192,256]{1,0:T(8,128)(2,1)S(1)} %pad_maximum_fusion.refs_3_), channel_id=1, source_target_pairs={{0,8},{8,16},{16,24},{24,32},{32,40},{40,48},{48,56},{56,64},{64,7... | collective-permute-start | bytes 294920 | tf_op jit(solution)/shard_map/ppermute | solution.py:205
  3.9 4.8 %collective-permute-done = bf16[192,256]{1,0:T(8,128)(2,1)S(1)} collective-permute-done((bf16[192,256]{1,0:T(8,128)(2,1)S(1)}, bf16[192,256]{1,0:T(8,128)(2,1)S(1)}, u32[]{:S(2)}, u32[]{:S(2)}) %collective-permute-start) | collective-permute-done | bytes 98336 | tf_op jit(solution)/shard_map/ppermute | solution.py:205
  8.6 1.0 broadcast_select_fusion.1
  9.6 7.5 %all-to-all-start = ((bf16[8,192,256]{2,1,0:T(8,128)(2,1)}), bf16[8,192,256]{2,1,0:T(8,128)(2,1)S(1)}, u32[]{:S(2)}, u32[]{:S(2)}) async-start(bf16[8,192,256]{2,1,0:T(8,128)(2,1)} %broadcast_select_fusion.1), calls=%async_computation | async-start | bytes 1572864 | tf_op jit(solution)/shard_map/all_to_all | solution.py:225
  17.1 1.9 %collective-permute-start.1 = (bf16[192,256]{1,0:T(8,128)(2,1)S(1)}, bf16[192,256]{1,0:T(8,128)(2,1)S(1)}, u32[]{:S(2)}, u32[]{:S(2)}) collective-permute-start(bf16[192,256]{1,0:T(8,128)(2,1)S(1)} %collective-permute-done), channel_id=1, source_target_pairs={{0,8},{8,16},{16,24},{24,32},{32,40},{40,48},{48,56},{56,64},{64,7... | collective-permute-start | bytes 294920 | tf_op jit(solution)/shard_map/ppermute | solution.py:205
  19.0 5.8 %collective-permute-done.1 = bf16[192,256]{1,0:T(8,128)(2,1)S(1)} collective-permute-done((bf16[192,256]{1,0:T(8,128)(2,1)S(1)}, bf16[192,256]{1,0:T(8,128)(2,1)S(1)}, u32[]{:S(2)}, u32[]{:S(2)}) %collective-permute-start.1) | collective-permute-done | bytes 98336 | tf_op jit(solution)/shard_map/ppermute | solution.py:205
  24.8 1.0 broadcast_select_fusion
  25.8 2.4 %all-to-all-done = bf16[8,192,256]{2,1,0:T(8,128)(2,1)S(1)} async-done(((bf16[8,192,256]{2,1,0:T(8,128)(2,1)}), bf16[8,192,256]{2,1,0:T(8,128)(2,1)S(1)}, u32[]{:S(2)}, u32[]{:S(2)}) %all-to-all-start) | async-done | bytes 786464 | tf_op jit(solution)/shard_map/all_to_all | solution.py:225
  28.2 4.9 %all-to-all-start.1 = ((bf16[8,192,256]{2,1,0:T(8,128)(2,1)}), bf16[8,192,256]{2,1,0:T(8,128)(2,1)S(1)}, u32[]{:S(2)}, u32[]{:S(2)}) async-start(bf16[8,192,256]{2,1,0:T(8,128)(2,1)} %broadcast_select_fusion), calls=%async_computation.1 | async-start | bytes 1572864 | tf_op jit(solution)/shard_map/all_to_all | solution.py:227
  33.2 0.0 copy-done.1
  33.2 0.0 copy-done
  33.2 37.3 %shard_map.46 = (f32[3072,256]{1,0:T(8,128)}, f32[2]{0:T(128)S(1)}) custom-call(s32[16]{0:T(128)S(1)} %copy-done.1, bf16[192,2048]{1,0:T(8,128)(2,1)S(1)} %copy-done, bf16[1536,256]{1,0:T(8,128)(2,1)S(1)} %bitcast.2, bf16[192,256]{1,0:T(8,128)(2,1)S(1)} %pad_maximum_fusion.refs_3_), custom_call_target="tpu_custom_call" | custom-call | flops 5435817984 | bytes 3932160 | tf_op jit(solution)/shard_map/pallas_call | solution.py:182
  70.5 0.0 all-to-all-done.1
  70.5 33.0 %shard_map.47 = bf16[192,2048]{1,0:T(8,128)(2,1)} custom-call(s32[16]{0:T(128)S(1)} %copy-done.1, f32[2]{0:T(128)S(1)} %get-tuple-element.10.refs_1_, bf16[192,2048]{1,0:T(8,128)(2,1)S(1)} %copy-done, bf16[1536,256]{1,0:T(8,128)(2,1)S(1)} %bitcast.3, f32[3072,256]{1,0:T(8,128)} %get-tuple-element.12.refs_4_), custom_call_target="tpu_custom_call" | custom-call | flops 4831838208 | bytes 3932160 | tf_op jit(solution)/shard_map/pallas_call | solution.py:182
  (1 shorter events, 0.0 us)
Async XLA Ops:
  0.0 33.2 %copy-start.1 = (s32[16]{0:T(128)S(1)}, s32[16]{0:T(128)}, u32[]{:S(2)}) copy-start(s32[16]{0:T(128)} %refs_0_.3) | copy-start | bytes 196
  0.0 33.2 %copy-start = (bf16[192,2048]{1,0:T(8,128)(2,1)S(1)}, bf16[192,2048]{1,0:T(8,128)(2,1)}, u32[]{:S(2)}) copy-start(bf16[192,2048]{1,0:T(8,128)(2,1)} %refs_2_.1) | copy-start | bytes 2359300
  0.9 7.7 %collective-permute-start = (bf16[192,256]{1,0:T(8,128)(2,1)S(1)}, bf16[192,256]{1,0:T(8,128)(2,1)S(1)}, u32[]{:S(2)}, u32[]{:S(2)}) collective-permute-start(bf16[192,256]{1,0:T(8,128)(2,1)S(1)} %pad_maximum_fusion.refs_3_), channel_id=1, source_target_pairs={{0,8},{8,16},{16,24},{24,32},{32,40},{40,48},{48,56},{56,64},{64,7... | collective-permute-start | bytes 294920 | tf_op jit(solution)/shard_map/ppermute | solution.py:205
  9.6 18.6 %all-to-all-start = ((bf16[8,192,256]{2,1,0:T(8,128)(2,1)}), bf16[8,192,256]{2,1,0:T(8,128)(2,1)S(1)}, u32[]{:S(2)}, u32[]{:S(2)}) async-start(bf16[8,192,256]{2,1,0:T(8,128)(2,1)} %broadcast_select_fusion.1), calls=%async_computation | async-start | bytes 1572864 | tf_op jit(solution)/shard_map/all_to_all | solution.py:225
  17.1 7.7 %collective-permute-start.1 = (bf16[192,256]{1,0:T(8,128)(2,1)S(1)}, bf16[192,256]{1,0:T(8,128)(2,1)S(1)}, u32[]{:S(2)}, u32[]{:S(2)}) collective-permute-start(bf16[192,256]{1,0:T(8,128)(2,1)S(1)} %collective-permute-done), channel_id=1, source_target_pairs={{0,8},{8,16},{16,24},{24,32},{32,40},{40,48},{48,56},{56,64},{64,7... | collective-permute-start | bytes 294920 | tf_op jit(solution)/shard_map/ppermute | solution.py:205
  28.2 42.3 %all-to-all-start.1 = ((bf16[8,192,256]{2,1,0:T(8,128)(2,1)}), bf16[8,192,256]{2,1,0:T(8,128)(2,1)S(1)}, u32[]{:S(2)}, u32[]{:S(2)}) async-start(bf16[8,192,256]{2,1,0:T(8,128)(2,1)} %broadcast_select_fusion), calls=%async_computation.1 | async-start | bytes 1572864 | tf_op jit(solution)/shard_map/all_to_all | solution.py:227

commit v4 on v3

v4 whole, which is shorter than its diff:
```python
from functools import partial

import jax
import jax.numpy as jnp
from jax import lax
from jax.experimental import pallas as pl
from jax.experimental.pallas import tpu as pltpu
from jax.sharding import PartitionSpec as P

HD = 128
SUB = 2
VMEM_BYTES = (52 * 2**20, 50 * 2**20, 50 * 2**20)
PARTS = 2
CUT = 128
TILE = 512
SCALE = HD**-0.5 * 1.4426950408889634
SAFE = 100.0
FAR = -(2.0**100)

bf16 = jnp.bfloat16
f32 = jnp.float32


def product(a, b, dims):
    return lax.dot_general(a, b, (dims, ((), ())), preferred_element_type=f32)


def largest_norm(x):
    squares = (x.astype(f32) * x.astype(f32)).astype(bf16)
    sums = product(squares, jnp.ones((HD, HD), bf16), ((1,), (0,)))
    return jnp.max(sums) * 1.02


def kernel(stage, back, ring, *refs):
    lengths, *refs = refs
    if stage:
        guard_in, *refs = refs
    q_ref, *refs = refs
    kv_refs, refs = refs[: len(back) or 1], refs[len(back) or 1 :]
    states, refs = (refs[:2], refs[2:]) if stage == 2 else ([], refs)
    out_hbm, *refs = refs
    if stage < 2:
        guard_out, *refs = refs
    state_ref, held_ref, out_ref, kx, vx, sems = refs
    keys = kx.shape[0]
    rows, width = q_ref.shape
    heads = width // HD
    size = SUB * rows
    block, part = lax.axis_index("qctx"), lax.axis_index("kctx")

    def copy_out(i):
        if stage < 2:
            here = pl.ds(i * (heads // PARTS) * rows, heads // PARTS * rows)
            return pltpu.make_async_copy(state_ref.at[0, here], out_hbm.at[here], sems.at[i])
        here = pl.ds(i * (width // PARTS), width // PARTS)
        return pltpu.make_async_copy(out_ref.at[:, here], out_hbm.at[:, here], sems.at[i])

    get_states = [
        pltpu.make_async_copy(state, state_ref.at[n], sems.at[PARTS + n]) for n, state in enumerate(states)
    ]
    for get in get_states:
        get.start()

    lane = lax.broadcasted_iota(jnp.int32, (1, HD), 1)
    starts = jnp.zeros((1, HD), jnp.int32)
    ends = jnp.zeros((1, HD), jnp.int32)
    run = jnp.int32(0)
    for d in range(lengths.shape[0]):
        starts = jnp.where(lane == d, run, starts)
        run = run + lengths[d]
        ends = jnp.where(lane == d, run, ends)
    at = lax.broadcasted_iota(jnp.int32, (rows, HD), 0) + block * ring + part * rows
    mine = (at >= starts) & (at < ends)
    onehot = jnp.where(mine, 1.0, 0.0).astype(bf16)
    if stage == 0:
        kx[:, HD:] = jnp.where(mine, 0.0, FAR).astype(bf16)
    row = 0
    for kv_ref, (slabs, offset) in zip(kv_refs, back):
        slots = ring // rows
        count = kv_ref.shape[0] // slots
        for j in range(slots):
            base = (block - slabs) * ring + j * rows + offset - jnp.where(j >= part, ring, 0)
            pos = lax.broadcasted_iota(jnp.int32, (count, HD), 0) + base
            apart = jnp.where((pos >= starts) & (pos < ends), 0.0, FAR)
            kx[row + j * count : row + (j + 1) * count, HD:] = apart.astype(bf16)
        row += kv_ref.shape[0]
    row = 0
    knorm = f32(0.0)
    for kv_ref in kv_refs:
        here = slice(row, row + kv_ref.shape[0])
        kx[here, 0:HD] = kv_ref[:, 0:HD]
        vx[here, 0:HD] = kv_ref[:, HD:]
        knorm = jnp.maximum(knorm, largest_norm(kv_ref[:, 0:HD]))
        row += kv_ref.shape[0]
    vx[:, HD:] = jnp.ones((keys, HD), bf16)
    if stage == 0:
        qnorm = largest_norm(q_ref[:, 0:HD])
        for h in range(1, heads):
            qnorm = jnp.maximum(qnorm, largest_norm(q_ref[:, h * HD : (h + 1) * HD]))
    else:
        qnorm = guard_in[1]
    plain = qnorm * knorm <= (SAFE / SCALE) ** 2
    if stage:
        plain = plain & (guard_in[0] == 1.0)
    if stage < 2:
        guard_out[0] = plain.astype(f32)
        guard_out[1] = qnorm

    def scores(q, key, count):
        s = product(q, kx[key : key + count, :], ((1,), (1,))) * SCALE
        if stage == 0:
            r = lax.broadcasted_iota(jnp.int32, (rows, count), 0)
            c = lax.broadcasted_iota(jnp.int32, (rows, count), 1) + key
            s = jnp.where(jnp.concatenate([c <= r] * (q.shape[0] // rows), axis=0), s, FAR)
        return s

    tiles = [(key, min(TILE, keys - key)) for key in range(0, keys, TILE)]

    def divided(part):
        total = jnp.broadcast_to(part[:, HD : HD + 1], (rows, HD))
        return (part[:, 0:HD] / total).astype(bf16)

    def update_of(head):
        q = [jnp.concatenate([q_ref[:, h * HD : (h + 1) * HD], onehot], axis=1) for h in range(head, head + SUB)]
        q = jnp.concatenate(q, axis=0)
        total = None
        for key, count in tiles:
            weights = jnp.exp2(scores(q, key, count)).astype(bf16)
            update = product(weights, vx[key : key + count, :], ((1,), (0,)))
            total = update if total is None else total + update
        return total

    def finish(head, update):
        here = slice(head * rows, head * rows + size)
        state = state_ref[0, here, :] + state_ref[1, here, :] + update
        for n in range(SUB):
            column = (head + n) * HD
            out_ref[:, column : column + HD] = divided(state[n * rows : (n + 1) * rows])

    for i in range(PARTS):
        group = range(i * heads // PARTS, (i + 1) * heads // PARTS, SUB)
        for head in group:
            here = slice(head * rows, head * rows + size)
            if stage < 2:
                update = update_of(head)
                lanes = lax.broadcasted_iota(jnp.int32, update.shape, 1)
                state_ref[0, here, :] = jnp.where(lanes == 2 * HD - 1, 0.0, update)
            elif i == 0:
                held_ref[here, :] = update_of(head)
            else:
                finish(head, update_of(head))
        if stage == 2 and i == 0:
            for get in get_states:
                get.wait()
            for head in group:
                finish(head, held_ref[head * rows : head * rows + size, :])
        copy_out(i).start()
    for i in range(PARTS):
        copy_out(i).wait()

    @pl.when(jnp.logical_not(plain))
    def _():
        def one(head, carry):
            row = pl.multiple_of(head * rows, rows)
            column = pl.multiple_of(head * HD, HD)
            lanes = lax.broadcasted_iota(jnp.int32, (rows, 2 * HD), 1)
            last_lane = lanes == 2 * HD - 1
            if stage < 2:
                state = jnp.where(last_lane, FAR, 0.0)
            else:
                one_state, other = state_ref[0, pl.ds(row, rows), :], state_ref[1, pl.ds(row, rows), :]
                tops = one_state[:, 2 * HD - 1 :], other[:, 2 * HD - 1 :]
                top = jnp.maximum(*tops)
                state = one_state * jnp.exp2(tops[0] - top) + other * jnp.exp2(tops[1] - top)
                state = jnp.where(last_lane, top, state)
            q = jnp.concatenate([q_ref[:, pl.ds(column, HD)], onehot], axis=1)
            for key, count in tiles:
                s = scores(q, key, count)
                old = state[:, 2 * HD - 1 :]
                top = jnp.maximum(old, jnp.max(s, axis=1, keepdims=True))
                weights = jnp.exp2(s - top).astype(bf16)
                update = product(weights, vx[key : key + count, :], ((1,), (0,)))
                state = state * jnp.exp2(old - top) + update
                state = jnp.where(last_lane, top, state)
            if stage < 2:
                state_ref[0, pl.ds(row, rows), :] = state
            else:
                out_ref[:, pl.ds(column, HD)] = divided(state)
            return carry

        lax.fori_loop(0, heads, one, 0)
        for i in range(PARTS):
            copy_out(i).start()
        for i in range(PARTS):
            copy_out(i).wait()


def attend(stage, back, ring, doc_lengths, guard, queries, kvs, states):
    rows, width = queries.shape
    keys = sum(kv.shape[0] for kv in kvs)
    heads = width // HD
    smem = pl.BlockSpec(memory_space=pltpu.SMEM)
    vmem = pl.BlockSpec(memory_space=pltpu.VMEM)
    hbm = pl.BlockSpec(memory_space=pltpu.HBM)
    guards = [guard] if stage else []
    args = [doc_lengths] + guards + [queries] + kvs + states
    in_specs = [smem] * (1 + len(guards)) + [vmem] * (1 + len(kvs)) + [hbm] * len(states)
    if stage < 2:
        out_shape = [jax.ShapeDtypeStruct((heads * rows, 2 * HD), f32), jax.ShapeDtypeStruct((2,), f32)]
        out_specs = [hbm, smem]
    else:
        out_shape = jax.ShapeDtypeStruct(queries.shape, bf16)
        out_specs = hbm
    return pl.pallas_call(
        partial(kernel, stage, back, ring),
        out_shape=out_shape,
        in_specs=in_specs,
        out_specs=out_specs,
        scratch_shapes=[
            pltpu.VMEM((1 if stage < 2 else 2, heads * rows, 2 * HD), f32),
            pltpu.VMEM((8, HD) if stage < 2 else (heads * rows // PARTS, 2 * HD), f32),
            pltpu.VMEM((16, HD) if stage < 2 else (rows, width), bf16),
            pltpu.VMEM((keys, 2 * HD), bf16),
            pltpu.VMEM((keys, 2 * HD), bf16),
            pltpu.SemaphoreType.DMA((PARTS + 2,)),
        ],
        compiler_params=pltpu.CompilerParams(vmem_limit_bytes=VMEM_BYTES[stage]),
        cost_estimate=pl.CostEstimate(
            flops=8 * heads * rows * keys * HD,
            bytes_accessed=2 * rows * width + heads * rows * HD * 8,
            transcendentals=heads * rows * keys,
        ),
    )(*args)


def passed_along(x, by):
    count = lax.axis_size("qctx")
    return lax.ppermute(x, "qctx", [(i, i + by) for i in range(count - by)])


def to_parts(upward, downward):
    fine = lax.axis_size("kctx")
    later = jnp.arange(fine)[:, None, None] > lax.axis_index("kctx")
    return jnp.where(later, upward[None], downward[None])


def beside(keys, values):
    low = jnp.array(-jnp.inf, bf16)
    keys = lax.pad(keys, low, ((0, 0, 0), (0, HD, 0)))
    return jnp.maximum(keys, lax.pad(values, low, ((0, 0, 0), (HD, 0, 0))))


def shards(queries, keys, values, doc_lengths):
    ring = lax.axis_size("kctx") * queries.shape[0]
    flat = lambda x: x.reshape(-1, 2 * HD)
    own = beside(keys, values)
    one_back = passed_along(own, 1)
    near_parts, held = lax.optimization_barrier((to_parts(own, one_back), one_back))
    near = lax.all_to_all(near_parts, "kctx", 0, 0)
    two_back = passed_along(held, 1)
    far_parts = to_parts(held[:CUT], two_back[:CUT])
    own_state, guard = attend(0, (), ring, doc_lengths, None, queries, [own], [])
    far_parts, guard = lax.optimization_barrier((far_parts, guard))
    far = lax.all_to_all(far_parts, "kctx", 0, 0)
    rest = passed_along(near[:, CUT:], 1)
    near_state, guard = attend(1, ((0, 0),), ring, doc_lengths, guard, queries, [flat(near)], [])
    far_rings = ((1, 0), (1, CUT))
    return attend(
        2, far_rings, ring, doc_lengths, guard, queries, [flat(far), flat(rest)], [own_state, near_state]
    )


def solution(mesh):
    placed = P(("qctx", "kctx"), "head")
    return jax.shard_map(
        shards, mesh=mesh, in_specs=(placed, placed, placed, P()), out_specs=placed, check_vma=False
    )
```

time: 104 us -> 116 us (1.12)
  the two profiles are of different devices: /device:TPU:258 before, /device:TPU:194 now
where the time goes in v4:
time: 116 us; the launch traced here: 115 us
  Pallas kernels  79 us (68%)
  starting transfers between devices  28.7 us (25%)
  other arithmetic  2.75 us (2%)
  waiting for transfers between devices  2.67 us (2%)
  local copies, waits for them, and re-layouts  1.82 us (2%)
    pallas_call x3, Pallas kernels, attend(): pl.pallas_call(partial(kernel, stage, back, ring), out_shape=out_shape, i...  79 us
    ppermute x3, starting transfers between devices, passed_along(): return lax.ppermute(x, 'qctx', [(i, i + by) for i in range(count - by)])  13.9 us
    all_to_all x1, starting transfers between devices, shards(): near = lax.all_to_all(near_parts, 'kctx', 0, 0)  7.59 us
    all_to_all x1, starting transfers between devices, shards(): far = lax.all_to_all(far_parts, 'kctx', 0, 0)  7.21 us
    ppermute x3, waiting for transfers between devices, passed_along(): return lax.ppermute(x, 'qctx', [(i, i + by) for i in range(count - by)])  2.67 us
  transfers between devices with their start and end apart: 5, of which 1 were waited for; matrix products, arithmetic and copies ran while one was open for 1% of the time, Pallas kernels for 40%

profile of v4, /device:TPU:194, one launch (start us, length us, event | category | flops | bytes accessed | tf_op | source)
XLA Modules:
  0.0 115.2 jit_solution(1421890725942393498)
XLA Ops:
  0.0 0.8 pad_maximum_fusion.refs_2_
  0.8 3.8 %collective-permute-start = (bf16[192,256]{1,0:T(8,128)(2,1)S(1)}, bf16[192,256]{1,0:T(8,128)(2,1)S(1)}, u32[]{:S(2)}, u32[]{:S(2)}) collective-permute-start(bf16[192,256]{1,0:T(8,128)(2,1)S(1)} %pad_maximum_fusion.refs_2_), channel_id=1, source_target_pairs={{0,8},{8,16},{16,24},{24,32},{32,40},{40,48},{48,56},{56,64},{64,7... | collective-permute-start | bytes 294920 | tf_op jit(solution)/shard_map/ppermute | solution.py:238
  4.7 2.7 %collective-permute-done = bf16[192,256]{1,0:T(8,128)(2,1)S(1)} collective-permute-done((bf16[192,256]{1,0:T(8,128)(2,1)S(1)}, bf16[192,256]{1,0:T(8,128)(2,1)S(1)}, u32[]{:S(2)}, u32[]{:S(2)}) %collective-permute-start) | collective-permute-done | bytes 98336 | tf_op jit(solution)/shard_map/ppermute | solution.py:238
  7.3 1.0 broadcast_select_fusion
  8.4 0.0 copy-start.1
  8.4 0.0 copy-start.3
  8.4 7.6 %all-to-all-start = ((bf16[8,192,256]{2,1,0:T(8,128)(2,1)}), bf16[8,192,256]{2,1,0:T(8,128)(2,1)S(1)}, u32[]{:S(2)}, u32[]{:S(2)}) async-start(bf16[8,192,256]{2,1,0:T(8,128)(2,1)} %broadcast_select_fusion), calls=%async_computation | async-start | bytes 1572864 | tf_op jit(solution)/shard_map/all_to_all | solution.py:259
  15.9 4.5 %collective-permute-start.1 = (bf16[192,256]{1,0:T(8,128)(2,1)S(1)}, bf16[192,256]{1,0:T(8,128)(2,1)S(1)}, u32[]{:S(2)}, u32[]{:S(2)}) collective-permute-start(bf16[192,256]{1,0:T(8,128)(2,1)S(1)} %collective-permute-done), channel_id=1, source_target_pairs={{0,8},{8,16},{16,24},{24,32},{32,40},{40,48},{48,56},{56,64},{64,7... | collective-permute-start | bytes 294920 | tf_op jit(solution)/shard_map/ppermute | solution.py:238
  20.5 0.0 copy-start
  20.5 1.1 copy-done
  21.6 0.0 copy-start.2
  21.6 0.7 copy-done.2
  22.3 14.2 %shard_map.46 = (f32[3072,256]{1,0:T(8,128)}, f32[2]{0:T(128)S(1)}) custom-call(s32[16]{0:T(128)S(1)} %copy-done.2, bf16[192,2048]{1,0:T(8,128)(2,1)S(1)} %copy-done, bf16[192,256]{1,0:T(8,128)(2,1)S(1)} %pad_maximum_fusion.refs_2_), custom_call_target="tpu_custom_call" | custom-call | flops 603979776 | bytes 3932160 | tf_op jit(solution)/shard_map/pallas_call | solution.py:214
  36.5 0.0 collective-permute-done.1
  36.5 0.9 broadcast_select_fusion.1
  37.4 0.0 all-to-all-done
  37.4 7.2 %all-to-all-start.1 = ((bf16[8,128,256]{2,1,0:T(8,128)(2,1)}), bf16[8,128,256]{2,1,0:T(8,128)(2,1)S(1)}, u32[]{:S(2)}, u32[]{:S(2)}) async-start(bf16[8,128,256]{2,1,0:T(8,128)(2,1)} %broadcast_select_fusion.1), calls=%async_computation.1 | async-start | bytes 1048576 | tf_op jit(solution)/shard_map/all_to_all | solution.py:264
  44.7 5.5 %collective-permute-start.2 = (bf16[8,64,256]{2,1,0:T(8,128)(2,1)S(1)}, bf16[8,64,256]{2,1,0:T(8,128)(2,1)S(1)}, u32[]{:S(2)}, u32[]{:S(2)}) collective-permute-start(bf16[8,64,256]{2,1,0:T(8,128)(2,1)S(1)} %slice.13), channel_id=1, source_target_pairs={{0,8},{8,16},{16,24},{24,32},{32,40},{40,48},{48,56},{56,64},{64,7... | collective-permute-start | bytes 786440 | tf_op jit(solution)/shard_map/ppermute | solution.py:238
  50.2 0.0 copy-done.1
  50.2 0.0 copy-done.3
  50.2 32.0 %shard_map.47 = (f32[3072,256]{1,0:T(8,128)}, f32[2]{0:T(128)S(1)}) custom-call(s32[16]{0:T(128)S(1)} %copy-done.3, f32[2]{0:T(128)S(1)} %get-tuple-element.15.refs_1_, bf16[192,2048]{1,0:T(8,128)(2,1)S(1)} %copy-done.1, bf16[1536,256]{1,0:T(8,128)(2,1)S(1)} %bitcast.3), custom_call_target="tpu_custom_call" | custom-call | flops 4831838208 | bytes 3932160 | tf_op jit(solution)/shard_map/pallas_call | solution.py:214
  82.2 0.0 all-to-all-done.1
  82.2 0.0 collective-permute-done.2
  82.2 32.8 %shard_map.48 = bf16[192,2048]{1,0:T(8,128)(2,1)} custom-call(s32[16]{0:T(128)S(1)} %copy-done.3, f32[2]{0:T(128)S(1)} %get-tuple-element.17.refs_1_, bf16[192,2048]{1,0:T(8,128)(2,1)S(1)} %copy-done.1, bf16[1024,256]{1,0:T(8,128)(2,1)S(1)} %bitcast.4, bf16[512,256]{1,0:T(8,128)(2,1)S(1)} %bitcast.5, f32[3072,256]{1,0:T(8,128)} %get-tuple-element.19.refs_5_, ...), custom_call_target="tpu_custom_call" | custom-call | flops 4831838208 | bytes 3932160 | tf_op jit(solution)/shard_map/pallas_call | solution.py:214
  (4 shorter events, 0.0 us)
Async XLA Ops:
  0.8 6.5 %collective-permute-start = (bf16[192,256]{1,0:T(8,128)(2,1)S(1)}, bf16[192,256]{1,0:T(8,128)(2,1)S(1)}, u32[]{:S(2)}, u32[]{:S(2)}) collective-permute-start(bf16[192,256]{1,0:T(8,128)(2,1)S(1)} %pad_maximum_fusion.refs_2_), channel_id=1, source_target_pairs={{0,8},{8,16},{16,24},{24,32},{32,40},{40,48},{48,56},{56,64},{64,7... | collective-permute-start | bytes 294920 | tf_op jit(solution)/shard_map/ppermute | solution.py:238
  8.4 41.9 %copy-start.1 = (bf16[192,2048]{1,0:T(8,128)(2,1)S(1)}, bf16[192,2048]{1,0:T(8,128)(2,1)}, u32[]{:S(2)}) copy-start(bf16[192,2048]{1,0:T(8,128)(2,1)} %refs_2_.3) | copy-start | bytes 2359300
  8.4 41.9 %copy-start.3 = (s32[16]{0:T(128)S(1)}, s32[16]{0:T(128)}, u32[]{:S(2)}) copy-start(s32[16]{0:T(128)} %refs_0_.5) | copy-start | bytes 196
  8.4 29.1 %all-to-all-start = ((bf16[8,192,256]{2,1,0:T(8,128)(2,1)}), bf16[8,192,256]{2,1,0:T(8,128)(2,1)S(1)}, u32[]{:S(2)}, u32[]{:S(2)}) async-start(bf16[8,192,256]{2,1,0:T(8,128)(2,1)} %broadcast_select_fusion), calls=%async_computation | async-start | bytes 1572864 | tf_op jit(solution)/shard_map/all_to_all | solution.py:259
  15.9 20.6 %collective-permute-start.1 = (bf16[192,256]{1,0:T(8,128)(2,1)S(1)}, bf16[192,256]{1,0:T(8,128)(2,1)S(1)}, u32[]{:S(2)}, u32[]{:S(2)}) collective-permute-start(bf16[192,256]{1,0:T(8,128)(2,1)S(1)} %collective-permute-done), channel_id=1, source_target_pairs={{0,8},{8,16},{16,24},{24,32},{32,40},{40,48},{48,56},{56,64},{64,7... | collective-permute-start | bytes 294920 | tf_op jit(solution)/shard_map/ppermute | solution.py:238
  20.5 1.1 copy-start
  21.6 0.7 copy-start.2
  37.4 44.7 %all-to-all-start.1 = ((bf16[8,128,256]{2,1,0:T(8,128)(2,1)}), bf16[8,128,256]{2,1,0:T(8,128)(2,1)S(1)}, u32[]{:S(2)}, u32[]{:S(2)}) async-start(bf16[8,128,256]{2,1,0:T(8,128)(2,1)} %broadcast_select_fusion.1), calls=%async_computation.1 | async-start | bytes 1048576 | tf_op jit(solution)/shard_map/all_to_all | solution.py:264
  44.7 37.5 %collective-permute-start.2 = (bf16[8,64,256]{2,1,0:T(8,128)(2,1)S(1)}, bf16[8,64,256]{2,1,0:T(8,128)(2,1)S(1)}, u32[]{:S(2)}, u32[]{:S(2)}) collective-permute-start(bf16[8,64,256]{2,1,0:T(8,128)(2,1)S(1)} %slice.13), channel_id=1, source_target_pairs={{0,8},{8,16},{16,24},{24,32},{32,40},{40,48},{48,56},{56,64},{64,7... | collective-permute-start | bytes 786440 | tf_op jit(solution)/shard_map/ppermute | solution.py:238

commit v5 on v3

--- a/solution.py
+++ b/solution.py
@@ -36,12 +36,11 @@
         lengths, q_ref, kv_ref, own_ref, out_hbm, guard_out, *scratch = refs
     else:
         lengths, guard_in, q_ref, kv_ref, state_hbm, out_hbm, *scratch = refs
-    state_ref, out_ref, kx, vx, sems = scratch
+    state_ref, held_ref, out_ref, apart, sems = scratch
     keys = kv_ref.shape[0]
     rows, width = q_ref.shape
     heads = width // HD
     size = SUB * rows
-    every = keys + rows if first else keys
     block, part = lax.axis_index("qctx"), lax.axis_index("kctx")
 
     def copy_out(i):
@@ -63,22 +62,29 @@
         starts = jnp.where(lane == d, run, starts)
         run = run + lengths[d]
         ends = jnp.where(lane == d, run, ends)
-    at = lax.broadcasted_iota(jnp.int32, (keys, HD), 0)
-    pos = block * keys + at - jnp.where(at >= part * rows, keys, 0) - back * keys
-    kx[0:keys, HD:] = jnp.where((pos >= starts) & (pos < ends), 0.0, FAR).astype(bf16)
-    at = lax.broadcasted_iota(jnp.int32, (rows, HD), 0) + block * keys + part * rows
-    mine = (at >= starts) & (at < ends)
+    slots = keys // rows
+    at = lax.broadcasted_iota(jnp.int32, (rows, HD), 0)
+    query_start = block * keys + part * rows
+    mine = (at >= starts - query_start) & (at < ends - query_start)
     onehot = jnp.where(mine, 1.0, 0.0).astype(bf16)
-    vx[:, HD:] = jnp.ones((every, HD), bf16)
-    kx[0:keys, 0:HD] = kv_ref[:, 0:HD]
-    vx[0:keys, 0:HD] = kv_ref[:, HD:]
-    if not first:
-        get_state.wait()
+    for j in range(slots):
+        base = (block - back) * keys + j * rows - jnp.where(j >= part, keys, 0)
+        inside = (at >= starts - base) & (at < ends - base)
+        apart[j * rows : (j + 1) * rows, :] = jnp.where(inside, 0.0, FAR).astype(bf16)
+    if first:
+        apart[keys:, :] = jnp.where(mine, 0.0, FAR).astype(bf16)
+
+    def kv_rows(key, count):
+        return own_ref[...] if key == keys else kv_ref[key : key + count, :]
+
+    def wide_keys(key, count):
+        return jnp.concatenate([kv_rows(key, count)[:, 0:HD], apart[key : key + count, :]], axis=1)
+
+    def wide_values(key, count):
+        return jnp.concatenate([kv_rows(key, count)[:, HD:], jnp.ones((count, HD), bf16)], axis=1)
+
     knorm = largest_norm(kv_ref[:, 0:HD])
     if first:
-        kx[keys:, HD:] = jnp.where(mine, 0.0, FAR).astype(bf16)
-        kx[keys:, 0:HD] = own_ref[:, 0:HD]
-        vx[keys:, 0:HD] = own_ref[:, HD:]
         knorm = jnp.maximum(knorm, largest_norm(own_ref[:, 0:HD]))
         qnorm = largest_norm(q_ref[:, 0:HD])
         for h in range(1, heads):
@@ -93,7 +99,7 @@
         plain = plain & (guard_in[0] == 1.0)
 
     def scores(q, key, count):
-        s = product(q, kx[key : key + count, :], ((1,), (1,))) * SCALE
+        s = product(q, wide_keys(key, count), ((1,), (1,))) * SCALE
         if key == keys:
             r = lax.broadcasted_iota(jnp.int32, (rows, rows), 0)
             c = lax.broadcasted_iota(jnp.int32, (rows, rows), 1)
@@ -107,23 +113,38 @@
         total = jnp.broadcast_to(part[:, HD : HD + 1], (rows, HD))
         return (part[:, 0:HD] / total).astype(bf16)
 
+    def update_of(head):
+        q = [jnp.concatenate([q_ref[:, h * HD : (h + 1) * HD], onehot], axis=1) for h in range(head, head + SUB)]
+        q = jnp.concatenate(q, axis=0)
+        total = None
+        for key, count in tiles(TILE):
+            weights = jnp.exp2(scores(q, key, count)).astype(bf16)
+            update = product(weights, wide_values(key, count), ((1,), (0,)))
+            total = update if total is None else total + update
+        return total
+
+    def finish(head, state):
+        for n in range(SUB):
+            column = (head + n) * HD
+            out_ref[:, column : column + HD] = divided(state[n * rows : (n + 1) * rows])
+
     for i in range(PARTS):
-        for head in range(i * heads // PARTS, (i + 1) * heads // PARTS, SUB):
+        group = range(i * heads // PARTS, (i + 1) * heads // PARTS, SUB)
+        for head in group:
             here = slice(head * rows, head * rows + size)
-            group = range(head, head + SUB)
-            q = [jnp.concatenate([q_ref[:, h * HD : (h + 1) * HD], onehot], axis=1) for h in group]
-            q = jnp.concatenate(q, axis=0)
-            state = None if first else state_ref[here, :]
-            for key, count in tiles(TILE):
-                weights = jnp.exp2(scores(q, key, count)).astype(bf16)
-                update = product(weights, vx[key : key + count, :], ((1,), (0,)))
-                state = update if state is None else state + update
             if first:
+                state = update_of(head)
                 lanes = lax.broadcasted_iota(jnp.int32, state.shape, 1)
                 state_ref[here, :] = jnp.where(lanes == 2 * HD - 1, 0.0, state)
+            elif i == 0:
+                held_ref[here, :] = update_of(head)
             else:
-                for n, h in enumerate(group):
-                    out_ref[:, h * HD : (h + 1) * HD] = divided(state[n * rows : (n + 1) * rows])
+                finish(head, state_ref[here, :] + update_of(head))
+        if not first and i == 0:
+            get_state.wait()
+            for head in group:
+                here = slice(head * rows, head * rows + size)
+                finish(head, state_ref[here, :] + held_ref[here, :])
         copy_out(i).start()
     for i in range(PARTS):
         copy_out(i).wait()
@@ -144,7 +165,7 @@
                 old = state[:, 2 * HD - 1 :]
                 top = jnp.maximum(old, jnp.max(s, axis=1, keepdims=True))
                 weights = jnp.exp2(s - top).astype(bf16)
-                update = product(weights, vx[key : key + count, :], ((1,), (0,)))
+                update = product(weights, wide_values(key, count), ((1,), (0,)))
                 state = state * jnp.exp2(old - top) + update
                 state = jnp.where(lanes == 2 * HD - 1, top, state)
             if first:
@@ -186,9 +207,9 @@
         out_specs=out_specs,
         scratch_shapes=[
             pltpu.VMEM((heads * rows, 2 * HD), f32),
+            pltpu.VMEM((8, HD) if first else (heads * rows // PARTS, 2 * HD), f32),
             pltpu.VMEM((8, HD) if first else (rows, width), bf16),
-            pltpu.VMEM((every, 2 * HD), bf16),
-            pltpu.VMEM((every, 2 * HD), bf16),
+            pltpu.VMEM((every, HD), bf16),
             pltpu.SemaphoreType.DMA((PARTS + 1,)),
         ],
         compiler_params=pltpu.CompilerParams(vmem_limit_bytes=VMEM_BYTES),

time: 104 us -> 103 us (level)
  Pallas kernels: 70.3 us -> 69.1 us
    pallas_call x2, Pallas kernels: 70.3 us -> 69.1 us  [attend(): pl.pallas_call(partial(kernel, first, back), out_shape=out_shape, in_spec...]
where the time goes in v5:
time: 103 us; the launch traced here: 102 us
  Pallas kernels  69.1 us (67%)
  starting transfers between devices  17.2 us (17%)
  waiting for transfers between devices  13 us (13%)
  other arithmetic  2.93 us (3%)
    pallas_call x2, Pallas kernels, attend(): pl.pallas_call(partial(kernel, first, back), out_shape=out_shape, in_spec...  69.1 us
    ppermute x2, waiting for transfers between devices, passed_along(): return lax.ppermute(x, 'qctx', [(i, i + by) for i in range(count - by)])  10.6 us
    all_to_all x1, starting transfers between devices, shards(): near = lax.all_to_all(near_parts, 'kctx', 0, 0).reshape(block_rows, 2 * HD)  7.46 us
    all_to_all x1, starting transfers between devices, shards(): lax.all_to_all(to_parts(held, two_back), 'kctx', 0, 0)  4.93 us
    ppermute x2, starting transfers between devices, passed_along(): return lax.ppermute(x, 'qctx', [(i, i + by) for i in range(count - by)])  4.84 us
    all_to_all x1, waiting for transfers between devices, shards(): near = lax.all_to_all(near_parts, 'kctx', 0, 0).reshape(block_rows, 2 * HD)  2.41 us
  transfers between devices with their start and end apart: 4, of which 3 were waited for; matrix products, arithmetic and copies ran while one was open for 1% of the time, Pallas kernels for 36%

profile of v5, /device:TPU:258, one launch (start us, length us, event | category | flops | bytes accessed | tf_op | source)
XLA Modules:
  0.0 102.4 jit_solution(8888651667127230150)
XLA Ops:
  0.0 0.0 copy-start.1
  0.0 0.0 copy-start
  0.0 0.9 pad_maximum_fusion.refs_3_
  0.9 2.9 %collective-permute-start = (bf16[192,256]{1,0:T(8,128)(2,1)S(1)}, bf16[192,256]{1,0:T(8,128)(2,1)S(1)}, u32[]{:S(2)}, u32[]{:S(2)}) collective-permute-start(bf16[192,256]{1,0:T(8,128)(2,1)S(1)} %pad_maximum_fusion.refs_3_), channel_id=1, source_target_pairs={{0,8},{8,16},{16,24},{24,32},{32,40},{40,48},{48,56},{56,64},{64,7... | collective-permute-start | bytes 294920 | tf_op jit(solution)/shard_map/ppermute | solution.py:226
  3.9 4.8 %collective-permute-done = bf16[192,256]{1,0:T(8,128)(2,1)S(1)} collective-permute-done((bf16[192,256]{1,0:T(8,128)(2,1)S(1)}, bf16[192,256]{1,0:T(8,128)(2,1)S(1)}, u32[]{:S(2)}, u32[]{:S(2)}) %collective-permute-start) | collective-permute-done | bytes 98336 | tf_op jit(solution)/shard_map/ppermute | solution.py:226
  8.6 1.0 broadcast_select_fusion.1
  9.6 7.5 %all-to-all-start = ((bf16[8,192,256]{2,1,0:T(8,128)(2,1)}), bf16[8,192,256]{2,1,0:T(8,128)(2,1)S(1)}, u32[]{:S(2)}, u32[]{:S(2)}) async-start(bf16[8,192,256]{2,1,0:T(8,128)(2,1)} %broadcast_select_fusion.1), calls=%async_computation | async-start | bytes 1572864 | tf_op jit(solution)/shard_map/all_to_all | solution.py:246
  17.1 1.9 %collective-permute-start.1 = (bf16[192,256]{1,0:T(8,128)(2,1)S(1)}, bf16[192,256]{1,0:T(8,128)(2,1)S(1)}, u32[]{:S(2)}, u32[]{:S(2)}) collective-permute-start(bf16[192,256]{1,0:T(8,128)(2,1)S(1)} %collective-permute-done), channel_id=1, source_target_pairs={{0,8},{8,16},{16,24},{24,32},{32,40},{40,48},{48,56},{56,64},{64,7... | collective-permute-start | bytes 294920 | tf_op jit(solution)/shard_map/ppermute | solution.py:226
  19.0 5.8 %collective-permute-done.1 = bf16[192,256]{1,0:T(8,128)(2,1)S(1)} collective-permute-done((bf16[192,256]{1,0:T(8,128)(2,1)S(1)}, bf16[192,256]{1,0:T(8,128)(2,1)S(1)}, u32[]{:S(2)}, u32[]{:S(2)}) %collective-permute-start.1) | collective-permute-done | bytes 98336 | tf_op jit(solution)/shard_map/ppermute | solution.py:226
  24.8 1.0 broadcast_select_fusion
  25.8 2.4 %all-to-all-done = bf16[8,192,256]{2,1,0:T(8,128)(2,1)S(1)} async-done(((bf16[8,192,256]{2,1,0:T(8,128)(2,1)}), bf16[8,192,256]{2,1,0:T(8,128)(2,1)S(1)}, u32[]{:S(2)}, u32[]{:S(2)}) %all-to-all-start) | async-done | bytes 786464 | tf_op jit(solution)/shard_map/all_to_all | solution.py:246
  28.2 4.9 %all-to-all-start.1 = ((bf16[8,192,256]{2,1,0:T(8,128)(2,1)}), bf16[8,192,256]{2,1,0:T(8,128)(2,1)S(1)}, u32[]{:S(2)}, u32[]{:S(2)}) async-start(bf16[8,192,256]{2,1,0:T(8,128)(2,1)} %broadcast_select_fusion), calls=%async_computation.1 | async-start | bytes 1572864 | tf_op jit(solution)/shard_map/all_to_all | solution.py:248
  33.2 0.0 copy-done.1
  33.2 0.0 copy-done
  33.2 37.3 %shard_map.46 = (f32[3072,256]{1,0:T(8,128)}, f32[2]{0:T(128)S(1)}) custom-call(s32[16]{0:T(128)S(1)} %copy-done.1, bf16[192,2048]{1,0:T(8,128)(2,1)S(1)} %copy-done, bf16[1536,256]{1,0:T(8,128)(2,1)S(1)} %bitcast.2, bf16[192,256]{1,0:T(8,128)(2,1)S(1)} %pad_maximum_fusion.refs_3_), custom_call_target="tpu_custom_call" | custom-call | flops 5435817984 | bytes 3932160 | tf_op jit(solution)/shard_map/pallas_call | solution.py:203
  70.5 0.0 all-to-all-done.1
  70.5 31.8 %shard_map.47 = bf16[192,2048]{1,0:T(8,128)(2,1)} custom-call(s32[16]{0:T(128)S(1)} %copy-done.1, f32[2]{0:T(128)S(1)} %get-tuple-element.10.refs_1_, bf16[192,2048]{1,0:T(8,128)(2,1)S(1)} %copy-done, bf16[1536,256]{1,0:T(8,128)(2,1)S(1)} %bitcast.3, f32[3072,256]{1,0:T(8,128)} %get-tuple-element.12.refs_4_), custom_call_target="tpu_custom_call" | custom-call | flops 4831838208 | bytes 3932160 | tf_op jit(solution)/shard_map/pallas_call | solution.py:203
  (1 shorter events, 0.0 us)
Async XLA Ops:
  0.0 33.2 %copy-start.1 = (s32[16]{0:T(128)S(1)}, s32[16]{0:T(128)}, u32[]{:S(2)}) copy-start(s32[16]{0:T(128)} %refs_0_.3) | copy-start | bytes 196
  0.0 33.2 %copy-start = (bf16[192,2048]{1,0:T(8,128)(2,1)S(1)}, bf16[192,2048]{1,0:T(8,128)(2,1)}, u32[]{:S(2)}) copy-start(bf16[192,2048]{1,0:T(8,128)(2,1)} %refs_2_.1) | copy-start | bytes 2359300
  0.9 7.7 %collective-permute-start = (bf16[192,256]{1,0:T(8,128)(2,1)S(1)}, bf16[192,256]{1,0:T(8,128)(2,1)S(1)}, u32[]{:S(2)}, u32[]{:S(2)}) collective-permute-start(bf16[192,256]{1,0:T(8,128)(2,1)S(1)} %pad_maximum_fusion.refs_3_), channel_id=1, source_target_pairs={{0,8},{8,16},{16,24},{24,32},{32,40},{40,48},{48,56},{56,64},{64,7... | collective-permute-start | bytes 294920 | tf_op jit(solution)/shard_map/ppermute | solution.py:226
  9.6 18.6 %all-to-all-start = ((bf16[8,192,256]{2,1,0:T(8,128)(2,1)}), bf16[8,192,256]{2,1,0:T(8,128)(2,1)S(1)}, u32[]{:S(2)}, u32[]{:S(2)}) async-start(bf16[8,192,256]{2,1,0:T(8,128)(2,1)} %broadcast_select_fusion.1), calls=%async_computation | async-start | bytes 1572864 | tf_op jit(solution)/shard_map/all_to_all | solution.py:246
  17.1 7.7 %collective-permute-start.1 = (bf16[192,256]{1,0:T(8,128)(2,1)S(1)}, bf16[192,256]{1,0:T(8,128)(2,1)S(1)}, u32[]{:S(2)}, u32[]{:S(2)}) collective-permute-start(bf16[192,256]{1,0:T(8,128)(2,1)S(1)} %collective-permute-done), channel_id=1, source_target_pairs={{0,8},{8,16},{16,24},{24,32},{32,40},{40,48},{48,56},{56,64},{64,7... | collective-permute-start | bytes 294920 | tf_op jit(solution)/shard_map/ppermute | solution.py:226
  28.2 42.2 %all-to-all-start.1 = ((bf16[8,192,256]{2,1,0:T(8,128)(2,1)}), bf16[8,192,256]{2,1,0:T(8,128)(2,1)S(1)}, u32[]{:S(2)}, u32[]{:S(2)}) async-start(bf16[8,192,256]{2,1,0:T(8,128)(2,1)} %broadcast_select_fusion), calls=%async_computation.1 | async-start | bytes 1572864 | tf_op jit(solution)/shard_map/all_to_all | solution.py:248

commit v6 on v5

--- a/solution.py
+++ b/solution.py
@@ -8,11 +8,11 @@
 from jax.sharding import PartitionSpec as P
 
 HD = 128
-SUB = 2
+SUB = 4
 LEAN_TILE = 512
 VMEM_BYTES = 50 * 2**20
 PARTS = 2
-TILE = 512
+TILES = {True: 256, False: 1536}
 SCALE = HD**-0.5 * 1.4426950408889634
 SAFE = 100.0
 FAR = -(2.0**100)
@@ -117,7 +117,7 @@
         q = [jnp.concatenate([q_ref[:, h * HD : (h + 1) * HD], onehot], axis=1) for h in range(head, head + SUB)]
         q = jnp.concatenate(q, axis=0)
         total = None
-        for key, count in tiles(TILE):
+        for key, count in tiles(TILES[first]):
             weights = jnp.exp2(scores(q, key, count)).astype(bf16)
             update = product(weights, wide_values(key, count), ((1,), (0,)))
             total = update if total is None else total + update

time: 103 us -> 102 us (level)
  the two profiles are of different devices: /device:TPU:258 before, /device:TPU:386 now
where the time goes in v6:
time: 102 us
  Pallas kernels  68.7 us (67%)
  starting transfers between devices  17.2 us (17%)
  waiting for transfers between devices  13 us (13%)
  other arithmetic  2.93 us (3%)
    pallas_call x2, Pallas kernels, attend(): pl.pallas_call(partial(kernel, first, back), out_shape=out_shape, in_spec...  68.7 us
    ppermute x2, waiting for transfers between devices, passed_along(): return lax.ppermute(x, 'qctx', [(i, i + by) for i in range(count - by)])  10.6 us
    all_to_all x1, starting transfers between devices, shards(): near = lax.all_to_all(near_parts, 'kctx', 0, 0).reshape(block_rows, 2 * HD)  7.46 us
    all_to_all x1, starting transfers between devices, shards(): lax.all_to_all(to_parts(held, two_back), 'kctx', 0, 0)  4.93 us
    ppermute x2, starting transfers between devices, passed_along(): return lax.ppermute(x, 'qctx', [(i, i + by) for i in range(count - by)])  4.84 us
    all_to_all x1, waiting for transfers between devices, shards(): near = lax.all_to_all(near_parts, 'kctx', 0, 0).reshape(block_rows, 2 * HD)  2.41 us
  transfers between devices with their start and end apart: 4, of which 3 were waited for; matrix products, arithmetic and copies ran while one was open for 1% of the time, Pallas kernels for 36%

profile of v6, /device:TPU:386, one launch (start us, length us, event | category | flops | bytes accessed | tf_op | source)
XLA Modules:
  0.0 102.0 jit_solution(15649205775379869884)
XLA Ops:
  0.0 0.0 copy-start.1
  0.0 0.0 copy-start
  0.0 0.9 pad_maximum_fusion.refs_3_
  0.9 2.9 %collective-permute-start = (bf16[192,256]{1,0:T(8,128)(2,1)S(1)}, bf16[192,256]{1,0:T(8,128)(2,1)S(1)}, u32[]{:S(2)}, u32[]{:S(2)}) collective-permute-start(bf16[192,256]{1,0:T(8,128)(2,1)S(1)} %pad_maximum_fusion.refs_3_), channel_id=1, source_target_pairs={{0,8},{8,16},{16,24},{24,32},{32,40},{40,48},{48,56},{56,64},{64,7... | collective-permute-start | bytes 294920 | tf_op jit(solution)/shard_map/ppermute | solution.py:226
  3.9 4.8 %collective-permute-done = bf16[192,256]{1,0:T(8,128)(2,1)S(1)} collective-permute-done((bf16[192,256]{1,0:T(8,128)(2,1)S(1)}, bf16[192,256]{1,0:T(8,128)(2,1)S(1)}, u32[]{:S(2)}, u32[]{:S(2)}) %collective-permute-start) | collective-permute-done | bytes 98336 | tf_op jit(solution)/shard_map/ppermute | solution.py:226
  8.6 1.0 broadcast_select_fusion.1
  9.6 7.5 %all-to-all-start = ((bf16[8,192,256]{2,1,0:T(8,128)(2,1)}), bf16[8,192,256]{2,1,0:T(8,128)(2,1)S(1)}, u32[]{:S(2)}, u32[]{:S(2)}) async-start(bf16[8,192,256]{2,1,0:T(8,128)(2,1)} %broadcast_select_fusion.1), calls=%async_computation | async-start | bytes 1572864 | tf_op jit(solution)/shard_map/all_to_all | solution.py:246
  17.1 1.9 %collective-permute-start.1 = (bf16[192,256]{1,0:T(8,128)(2,1)S(1)}, bf16[192,256]{1,0:T(8,128)(2,1)S(1)}, u32[]{:S(2)}, u32[]{:S(2)}) collective-permute-start(bf16[192,256]{1,0:T(8,128)(2,1)S(1)} %collective-permute-done), channel_id=1, source_target_pairs={{0,8},{8,16},{16,24},{24,32},{32,40},{40,48},{48,56},{56,64},{64,7... | collective-permute-start | bytes 294920 | tf_op jit(solution)/shard_map/ppermute | solution.py:226
  19.0 5.8 %collective-permute-done.1 = bf16[192,256]{1,0:T(8,128)(2,1)S(1)} collective-permute-done((bf16[192,256]{1,0:T(8,128)(2,1)S(1)}, bf16[192,256]{1,0:T(8,128)(2,1)S(1)}, u32[]{:S(2)}, u32[]{:S(2)}) %collective-permute-start.1) | collective-permute-done | bytes 98336 | tf_op jit(solution)/shard_map/ppermute | solution.py:226
  24.8 1.0 broadcast_select_fusion
  25.8 2.4 %all-to-all-done = bf16[8,192,256]{2,1,0:T(8,128)(2,1)S(1)} async-done(((bf16[8,192,256]{2,1,0:T(8,128)(2,1)}), bf16[8,192,256]{2,1,0:T(8,128)(2,1)S(1)}, u32[]{:S(2)}, u32[]{:S(2)}) %all-to-all-start) | async-done | bytes 786464 | tf_op jit(solution)/shard_map/all_to_all | solution.py:246
  28.2 4.9 %all-to-all-start.1 = ((bf16[8,192,256]{2,1,0:T(8,128)(2,1)}), bf16[8,192,256]{2,1,0:T(8,128)(2,1)S(1)}, u32[]{:S(2)}, u32[]{:S(2)}) async-start(bf16[8,192,256]{2,1,0:T(8,128)(2,1)} %broadcast_select_fusion), calls=%async_computation.1 | async-start | bytes 1572864 | tf_op jit(solution)/shard_map/all_to_all | solution.py:248
  33.2 0.0 copy-done.1
  33.2 0.0 copy-done
  33.2 37.1 %shard_map.46 = (f32[3072,256]{1,0:T(8,128)}, f32[2]{0:T(128)S(1)}) custom-call(s32[16]{0:T(128)S(1)} %copy-done.1, bf16[192,2048]{1,0:T(8,128)(2,1)S(1)} %copy-done, bf16[1536,256]{1,0:T(8,128)(2,1)S(1)} %bitcast.2, bf16[192,256]{1,0:T(8,128)(2,1)S(1)} %pad_maximum_fusion.refs_3_), custom_call_target="tpu_custom_call" | custom-call | flops 5435817984 | bytes 3932160 | tf_op jit(solution)/shard_map/pallas_call | solution.py:203
  70.3 0.0 all-to-all-done.1
  70.3 31.5 %shard_map.47 = bf16[192,2048]{1,0:T(8,128)(2,1)} custom-call(s32[16]{0:T(128)S(1)} %copy-done.1, f32[2]{0:T(128)S(1)} %get-tuple-element.10.refs_1_, bf16[192,2048]{1,0:T(8,128)(2,1)S(1)} %copy-done, bf16[1536,256]{1,0:T(8,128)(2,1)S(1)} %bitcast.3, f32[3072,256]{1,0:T(8,128)} %get-tuple-element.12.refs_4_), custom_call_target="tpu_custom_call" | custom-call | flops 4831838208 | bytes 3932160 | tf_op jit(solution)/shard_map/pallas_call | solution.py:203
  (1 shorter events, 0.0 us)
Async XLA Ops:
  0.0 33.2 %copy-start.1 = (s32[16]{0:T(128)S(1)}, s32[16]{0:T(128)}, u32[]{:S(2)}) copy-start(s32[16]{0:T(128)} %refs_0_.3) | copy-start | bytes 196
  0.0 33.2 %copy-start = (bf16[192,2048]{1,0:T(8,128)(2,1)S(1)}, bf16[192,2048]{1,0:T(8,128)(2,1)}, u32[]{:S(2)}) copy-start(bf16[192,2048]{1,0:T(8,128)(2,1)} %refs_2_.1) | copy-start | bytes 2359300
  0.9 7.7 %collective-permute-start = (bf16[192,256]{1,0:T(8,128)(2,1)S(1)}, bf16[192,256]{1,0:T(8,128)(2,1)S(1)}, u32[]{:S(2)}, u32[]{:S(2)}) collective-permute-start(bf16[192,256]{1,0:T(8,128)(2,1)S(1)} %pad_maximum_fusion.refs_3_), channel_id=1, source_target_pairs={{0,8},{8,16},{16,24},{24,32},{32,40},{40,48},{48,56},{56,64},{64,7... | collective-permute-start | bytes 294920 | tf_op jit(solution)/shard_map/ppermute | solution.py:226
  9.6 18.6 %all-to-all-start = ((bf16[8,192,256]{2,1,0:T(8,128)(2,1)}), bf16[8,192,256]{2,1,0:T(8,128)(2,1)S(1)}, u32[]{:S(2)}, u32[]{:S(2)}) async-start(bf16[8,192,256]{2,1,0:T(8,128)(2,1)} %broadcast_select_fusion.1), calls=%async_computation | async-start | bytes 1572864 | tf_op jit(solution)/shard_map/all_to_all | solution.py:246
  17.1 7.7 %collective-permute-start.1 = (bf16[192,256]{1,0:T(8,128)(2,1)S(1)}, bf16[192,256]{1,0:T(8,128)(2,1)S(1)}, u32[]{:S(2)}, u32[]{:S(2)}) collective-permute-start(bf16[192,256]{1,0:T(8,128)(2,1)S(1)} %collective-permute-done), channel_id=1, source_target_pairs={{0,8},{8,16},{16,24},{24,32},{32,40},{40,48},{48,56},{56,64},{64,7... | collective-permute-start | bytes 294920 | tf_op jit(solution)/shard_map/ppermute | solution.py:226
  28.2 42.1 %all-to-all-start.1 = ((bf16[8,192,256]{2,1,0:T(8,128)(2,1)}), bf16[8,192,256]{2,1,0:T(8,128)(2,1)S(1)}, u32[]{:S(2)}, u32[]{:S(2)}) async-start(bf16[8,192,256]{2,1,0:T(8,128)(2,1)} %broadcast_select_fusion), calls=%async_computation.1 | async-start | bytes 1572864 | tf_op jit(solution)/shard_map/all_to_all | solution.py:248
